TPU v7x, 512 devices: a whole 4x8x8 slice. The times are simulated.
512 devices in a mesh: prow: 16 (over z, core), pcol: 32 (over x, y).
Axes of the slice: x: 4, y: 8, z: 8, core: 2. Of those that a mesh axis runs over, the one named last changes fastest.
Arguments:
- right_side: bfloat16 [15, 2048, 640], P(None, 'pcol', 'prow'), may hold values from -6 to 6
- lower_panels: bfloat16 [34, 2048, 2048], P(None, 'pcol', 'prow'), may hold values from -0.09375 to 0.09375
- lower_pattern: int32 [34, 32, 32], P(None, 'pcol', 'prow'), may hold values 0 or 1
- upper_panels: bfloat16 [34, 2048, 2048], P(None, 'pcol', 'prow'), may hold values from -0.09375 to 0.09375
- upper_pattern: int32 [34, 32, 32], P(None, 'pcol', 'prow'), may hold values 0 or 1
- lower_inverse: bfloat16 [15, 2048, 2048], P(None, 'pcol', 'prow'), may hold values from -0.2 to 1.2, as said below
- upper_inverse: bfloat16 [15, 2048, 2048], P(None, 'pcol', 'prow'), may hold values from -0.2 to 1.2, as said below
Outputs:
- solution: bfloat16 [15, 2048, 640], P(None, 'pcol', 'prow')
Inputs may be any that keep to these rules, and one draw needn't show every extreme that they name: `lower_pattern`: 1 where a block of a panel is nonzero, 0 where it is empty. `upper_pattern`: 1 where a block of a panel is nonzero, 0 where it is empty. `lower_inverse`: the transpose of the given inverse of the diagonal block of each supernode of L. `upper_inverse`: the given inverse of the diagonal block of each supernode of U.
All inputs are finite; a program needn't handle non-finite values.
Results may differ from a plain program's by a relative error of at most 0.04.
Values may be sent and summed in bfloat16 or wider, within the bound.
No kernel may reach another device: no remote copies, remote signals or barrier semaphores. Data moves between devices by JAX's collectives and lax.ppermute only.
A program may use at most 64 MiB of HBM per device.

v0:
```python
import jax
import jax.numpy as jnp
from jax import lax
from jax.sharding import PartitionSpec as P

node_offsets = (0, 8, 12, 14)


def pair_offset(desc_level, anc_level):
    offset = 0
    for first_level in range(4):
        for second_level in range(first_level + 1, 4):
            if first_level == desc_level and second_level == anc_level:
                return offset
            offset = offset + 2 ** (3 - first_level)
    return offset


def apply_pattern(panels, pattern):
    amount, row_blocks, col_blocks = pattern.shape
    row_size = panels.shape[1] // row_blocks
    col_size = panels.shape[2] // col_blocks
    shaped = panels.reshape(amount, row_blocks, row_size, col_blocks, col_size)
    shaped = jnp.where(pattern[:, :, None, :, None] > 0, shaped, jnp.zeros((), panels.dtype))
    return shaped.reshape(panels.shape)


def gather_terms(panels, vectors, fanout):
    group_count = panels.shape[0] // fanout
    grouped = panels.reshape(group_count, fanout, panels.shape[1], panels.shape[2])
    stacked = vectors.reshape(group_count, fanout, vectors.shape[1], vectors.shape[2])
    return jnp.einsum("gfab,gfbr->gar", grouped, stacked, preferred_element_type=jnp.float32)


def spread_terms(panels, vectors, fanout):
    group_count = panels.shape[0] // fanout
    grouped = panels.reshape(group_count, fanout, panels.shape[1], panels.shape[2])
    spread = jnp.einsum("gfba,gbr->gfar", grouped, vectors, preferred_element_type=jnp.float32)
    return spread.reshape(panels.shape[0], panels.shape[2], vectors.shape[2])


def solve_all(right_side, lower_panels, upper_panels, lower_inverse, upper_inverse):
    forward = []
    for height in range(4):
        offset = node_offsets[height]
        amount = 2 ** (3 - height)
        source = right_side[offset : offset + amount]
        if height > 0:
            partial_value = None
            for desc_level in range(height):
                pair_first = pair_offset(desc_level, height)
                group_size = 2 ** (3 - desc_level)
                product = gather_terms(
                    lower_panels[pair_first : pair_first + group_size],
                    forward[desc_level],
                    2 ** (height - desc_level),
                )
                partial_value = product if partial_value is None else partial_value + product
            own_share = lax.psum_scatter(
                partial_value.astype(jnp.bfloat16), "prow", scatter_dimension=2, tiled=True
            ).astype(jnp.float32)
            residual_share = (source.astype(jnp.float32) - own_share).astype(jnp.bfloat16)
        else:
            residual_share = source
        residual = lax.all_gather(residual_share, "prow", axis=2, tiled=True)
        partial_value = jnp.einsum(
            "gba,gbr->gar",
            lower_inverse[offset : offset + amount],
            residual,
            preferred_element_type=jnp.float32,
        )
        forward.append(lax.psum(partial_value.astype(jnp.bfloat16), "pcol"))
    slot_count = forward[0].shape[2] // lax.axis_size("pcol")
    slot_start = lax.axis_index("pcol") * slot_count
    backward = [None, None, None, None]
    for height in (3, 2, 1, 0):
        offset = node_offsets[height]
        amount = 2 ** (3 - height)
        if height < 3:
            partial_value = None
            for anc_level in range(height + 1, 4):
                pair_first = pair_offset(height, anc_level)
                product = spread_terms(
                    upper_panels[pair_first : pair_first + amount],
                    backward[anc_level],
                    2 ** (anc_level - height),
                )
                partial_value = product if partial_value is None else partial_value + product
            own_share = lax.psum_scatter(
                partial_value.astype(jnp.bfloat16), "pcol", scatter_dimension=2, tiled=True
            ).astype(jnp.float32)
            solved_share = lax.dynamic_slice_in_dim(forward[height], slot_start, slot_count, 2)
            residual_share = (solved_share.astype(jnp.float32) - own_share).astype(jnp.bfloat16)
            residual = lax.all_gather(residual_share, "pcol", axis=2, tiled=True)
        else:
            residual = forward[height]
        partial_value = jnp.einsum(
            "gab,gbr->gar",
            upper_inverse[offset : offset + amount],
            residual,
            preferred_element_type=jnp.float32,
        )
        backward[height] = lax.psum(partial_value.astype(jnp.bfloat16), "prow")
    own_count = forward[0].shape[2] // lax.axis_size("prow")
    own_start = lax.axis_index("prow") * own_count
    pieces_out = [
        lax.dynamic_slice_in_dim(solved_level, own_start, own_count, 2) for solved_level in backward
    ]
    return jnp.concatenate(pieces_out, axis=0)


def local(
    right_side,
    lower_panels,
    lower_pattern,
    upper_panels,
    upper_pattern,
    lower_inverse,
    upper_inverse,
):
    masked_lower = apply_pattern(lower_panels, lower_pattern)
    masked_upper = apply_pattern(upper_panels, upper_pattern)
    return solve_all(right_side, masked_lower, masked_upper, lower_inverse, upper_inverse)


def solution(mesh):
    in_specs = (
        P(None, "pcol", "prow"),
        P(None, "pcol", "prow"),
        P(None, "pcol", "prow"),
        P(None, "pcol", "prow"),
        P(None, "pcol", "prow"),
        P(None, "pcol", "prow"),
        P(None, "pcol", "prow"),
    )
    out_specs = P(None, "pcol", "prow")
    return jax.shard_map(local, mesh=mesh, in_specs=in_specs, out_specs=out_specs, check_vma=False)
```

profile of v0, /device:TPU:1, one launch (start us, length us, event | category | flops | bytes accessed | tf_op | source)
XLA Modules:
  0.0 2177.3 jit_solution(12845593577522661912)
XLA Ops:
  7.5 28.1 %all_gather.21 = bf16[8,64,640]{1,2,0:T(8,128)(2,1)S(1)} all-gather(bf16[8,64,40]{1,2,0:T(8,128)(2,1)S(1)} %slice.85), channel_id=1, replica_groups=mesh['prow'=16,'pcol'=32] {'prow'}, dimensions={2}, use_global_device_ids=true | all-gather | bytes 696320 | tf_op jit(solution)/shard_map/all_gather | solution.py:65
  41.6 150.3 %all-reduce.17.cloned.1.call-done = bf16[8,128,640]{1,0,2:T(8,128)(2,1)} async-done(((bf16[8,128,640]{1,0,2:T(8,128)(2,1)}), bf16[8,128,640]{1,0,2:T(8,128)(2,1)}) %all-reduce.17.cloned.1.call-update) | async-done | bytes 1310736 | tf_op jit(solution)/shard_map/psum | solution.py:72
  195.5 59.2 %reduce-scatter.9.cloned.1.call-done = bf16[40,256]{1,0:T(8,128)(2,1)} async-done(((bf16[640,256]{1,0:T(8,128)(2,1)}), bf16[40,256]{1,0:T(8,128)(2,1)}) %reduce-scatter.9.cloned.1.call-update) | async-done | bytes 20496
  255.5 19.5 all_gather.22
  276.7 151.8 %all-reduce.19.cloned.1.call-done = bf16[4,128,640]{1,2,0:T(8,128)(2,1)} async-done(((bf16[4,128,640]{1,2,0:T(8,128)(2,1)}), bf16[4,128,640]{1,2,0:T(8,128)(2,1)}) %all-reduce.19.cloned.1.call-update) | async-done | bytes 655376 | tf_op jit(solution)/shard_map/psum | solution.py:72
  433.5 113.2 %all-reduce.33.cloned.1.call-done = bf16[2,64,640]{1,2,0:T(8,128)(2,1)} async-done(((bf16[2,64,640]{1,2,0:T(8,128)(2,1)}), bf16[2,64,640]{1,2,0:T(8,128)(2,1)}) %all-reduce.33.cloned.1.call-update) | async-done | bytes 163856
  547.4 15.6 all_gather.23
  565.0 150.2 %all-reduce.21.cloned.1.call-done = bf16[2,128,640]{1,2,0:T(8,128)(2,1)} async-done(((bf16[2,128,640]{1,2,0:T(8,128)(2,1)}), bf16[2,128,640]{1,2,0:T(8,128)(2,1)}) %all-reduce.21.cloned.1.call-update) | async-done | bytes 327696 | tf_op jit(solution)/shard_map/psum | solution.py:72
  717.2 109.3 %all-reduce.35.cloned.1.call-done = bf16[1,64,640]{2,1,0:T(8,128)(2,1)} async-done(((bf16[1,64,640]{2,1,0:T(8,128)(2,1)}), bf16[1,64,640]{2,1,0:T(8,128)(2,1)}) %all-reduce.35.cloned.1.call-update) | async-done | bytes 81936
  827.4 16.0 all_gather.24
  844.9 147.1 %all-reduce.23.cloned.1.call-done = bf16[128,640]{0,1:T(8,128)(2,1)} async-done(((bf16[128,640]{0,1:T(8,128)(2,1)}), bf16[128,640]{0,1:T(8,128)(2,1)}) %all-reduce.23.cloned.1.call-update) | async-done | bytes 163856 | tf_op jit(solution)/shard_map/psum | solution.py:72
  995.0 108.6 %all-reduce.25.cloned.1.call-done = bf16[1,64,640]{2,1,0:T(8,128)(2,1)} async-done(((bf16[1,64,640]{2,1,0:T(8,128)(2,1)}), bf16[1,64,640]{2,1,0:T(8,128)(2,1)}) %all-reduce.25.cloned.1.call-update) | async-done | bytes 81936 | tf_op jit(solution)/shard_map/psum | solution.py:103
  1107.9 150.0 %all-reduce.37.cloned.1.call-done = bf16[2,128,640]{1,0,2:T(2,128)(2,1)} async-done(((bf16[2,128,640]{1,0,2:T(2,128)(2,1)}), bf16[2,128,640]{1,0,2:T(2,128)(2,1)}) %all-reduce.37.cloned.1.call-update) | async-done | bytes 327696
  1259.3 35.7 %all_gather.25 = bf16[2,128,640]{1,0,2:T(2,128)(2,1)S(1)} all-gather(bf16[2,128,20]{1,0,2:T(2,128)(2,1)S(1)} %copy.47), channel_id=1, replica_groups=mesh['prow'=16,'pcol'=32] {'pcol'}, dimensions={2}, use_global_device_ids=true | all-gather | bytes 337920 | tf_op jit(solution)/shard_map/all_gather | solution.py:94
  1297.3 121.8 %all-reduce.27.cloned.1.call-done = bf16[2,64,640]{2,1,0:T(8,128)(2,1)} async-done(((bf16[2,64,640]{2,1,0:T(8,128)(2,1)}), bf16[2,64,640]{2,1,0:T(8,128)(2,1)}) %all-reduce.27.cloned.1.call-update) | async-done | bytes 163856 | tf_op jit(solution)/shard_map/psum | solution.py:103
  1425.5 150.5 %all-reduce.39.cloned.1.call-done = bf16[4,128,640]{1,0,2:T(4,128)(2,1)} async-done(((bf16[4,128,640]{1,0,2:T(4,128)(2,1)}), bf16[4,128,640]{1,0,2:T(4,128)(2,1)}) %all-reduce.39.cloned.1.call-update) | async-done | bytes 655376
  1576.8 37.1 %all_gather.26 = bf16[4,128,640]{1,0,2:T(4,128)(2,1)S(1)} all-gather(bf16[4,128,20]{1,0,2:T(4,128)(2,1)S(1)} %copy.52), channel_id=1, replica_groups=mesh['prow'=16,'pcol'=32] {'pcol'}, dimensions={2}, use_global_device_ids=true | all-gather | bytes 675840 | tf_op jit(solution)/shard_map/all_gather | solution.py:94
  1613.9 1.9 fusion.23
  1616.5 126.5 %all-reduce.29.cloned.1.call-done = bf16[4,64,640]{2,1,0:T(8,128)(2,1)} async-done(((bf16[4,64,640]{2,1,0:T(8,128)(2,1)}), bf16[4,64,640]{2,1,0:T(8,128)(2,1)}) %all-reduce.29.cloned.1.call-update) | async-done | bytes 327696 | tf_op jit(solution)/shard_map/psum | solution.py:103
  1745.2 1.9 copy.56
  1747.1 215.5 %reduce-scatter.7.cloned.1.call-done = bf16[8,128,20]{1,0,2:T(8,128)(2,1)} async-done(((bf16[8,128,640]{1,0,2:T(8,128)(2,1)}), bf16[8,128,20]{1,0,2:T(8,128)(2,1)}) %reduce-scatter.7.cloned.1.call-update) | async-done | bytes 40976 | tf_op jit(solution)/shard_map/reduce_scatter | solution.py:89
  1964.1 82.9 %all-gather.2.cloned.1.call-done = bf16[8,128,640]{1,0,2:T(8,128)(2,1)} async-done(((bf16[8,128,20]{1,0,2:T(8,128)(2,1)}), bf16[8,128,640]{1,0,2:T(8,128)(2,1)}) %all-gather.2.cloned.1.call-update) | async-done | bytes 1310736 | tf_op jit(solution)/shard_map/all_gather | solution.py:94
  2047.0 2.8 fusion.13
  2051.1 117.8 %all-reduce.31.cloned.1.call-done = bf16[8,64,640]{2,1,0:T(8,128)(2,1)} async-done(((bf16[8,64,640]{2,1,0:T(8,128)(2,1)}), bf16[8,64,640]{2,1,0:T(8,128)(2,1)}) %all-reduce.31.cloned.1.call-update) | async-done | bytes 655376 | tf_op jit(solution)/shard_map/psum | solution.py:103
  (130 shorter events, 49.1 us)
Async XLA Ops:
  6.5 185.4 %all-reduce.17.cloned.1.call-start = ((), (), s32[]{:S(2)}) async-start(), calls=%async_computation.2 | async-start | bytes 2621440 | tf_op jit(solution)/shard_map/psum | solution.py:72
  38.1 216.5 %reduce-scatter.9.cloned.1.call-start = ((), (), s32[]{:S(2)}) async-start(), calls=%async_computation.12 | async-start | bytes 348160
  193.7 61.8 %copy-start.10 = (bf16[15,64,40]{1,2,0:T(8,128)(2,1)S(1)}, bf16[15,64,40]{1,2,0:T(8,128)(2,1)}, u32[]{:S(2)}) copy-start(bf16[15,64,40]{1,2,0:T(8,128)(2,1)} %param.7) | copy-start | bytes 230404
  195.4 233.1 %all-reduce.19.cloned.1.call-start = ((), (), s32[]{:S(2)}) async-start(), calls=%async_computation.3 | async-start | bytes 1310720 | tf_op jit(solution)/shard_map/psum | solution.py:72
  276.2 153.7 %copy-start.1 = (bf16[8,128,640]{1,0,2:T(8,128)(2,1)S(1)}, bf16[8,128,640]{1,0,2:T(8,128)(2,1)}, u32[]{:S(2)}) copy-start(bf16[8,128,640]{1,0,2:T(8,128)(2,1)} %all-reduce.17.cloned.1.call-done) | copy-start | bytes 3932164
  276.2 270.5 %all-reduce.33.cloned.1.call-start = ((), (), s32[]{:S(2)}) async-start(), calls=%async_computation.13 | async-start | bytes 655360
  431.1 284.0 %all-reduce.21.cloned.1.call-start = ((), (), s32[]{:S(2)}) async-start(), calls=%async_computation.4 | async-start | bytes 655360 | tf_op jit(solution)/shard_map/psum | solution.py:72
  564.0 153.0 %slice-start = ((bf16[15,64,40]{1,2,0:T(8,128)(2,1)}), bf16[1,64,40]{1,2,0:T(8,128)(2,1)S(1)}, s32[]{:S(2)}) async-start(bf16[15,64,40]{1,2,0:T(8,128)(2,1)} %param.7), calls=%async_computation.17 | async-start | bytes 20480 | tf_op jit(solution)/shard_map/slice | solution.py:47
  564.1 262.4 %all-reduce.35.cloned.1.call-start = ((), (), s32[]{:S(2)}) async-start(), calls=%async_computation.14 | async-start | bytes 163840
  564.6 279.8 %copy-start.5 = (bf16[34,64,128]{2,1,0:T(8,128)(2,1)S(1)}, bf16[34,64,128]{2,1,0:T(8,128)(2,1)}, u32[]{:S(2)}) copy-start(bf16[34,64,128]{2,1,0:T(8,128)(2,1)} %param.10) | copy-start | bytes 1671172
  717.0 275.0 %all-reduce.23.cloned.1.call-start = ((), (), s32[]{:S(2)}) async-start(), calls=%async_computation.5 | async-start | bytes 327680 | tf_op jit(solution)/shard_map/psum | solution.py:72
  844.3 259.3 %all-reduce.25.cloned.1.call-start = ((), (), s32[]{:S(2)}) async-start(), calls=%async_computation.6 | async-start | bytes 163840 | tf_op jit(solution)/shard_map/psum | solution.py:103
  993.8 264.1 %all-reduce.37.cloned.1.call-start = ((), (), s32[]{:S(2)}) async-start(), calls=%async_computation.15 | async-start | bytes 655360
  1105.9 313.3 %all-reduce.27.cloned.1.call-start = ((), (), s32[]{:S(2)}) async-start(), calls=%async_computation.7 | async-start | bytes 327680 | tf_op jit(solution)/shard_map/psum | solution.py:103
  1296.7 123.8 %copy-start.2 = (bf16[1,64,640]{2,1,0:T(8,128)(2,1)S(1)}, bf16[1,64,640]{2,1,0:T(8,128)(2,1)}, u32[]{:S(2)}) copy-start(bf16[1,64,640]{2,1,0:T(8,128)(2,1)} %all-reduce.25.cloned.1.call-done) | copy-start | bytes 245764
  1296.7 279.3 %all-reduce.39.cloned.1.call-start = ((), (), s32[]{:S(2)}) async-start(), calls=%async_computation.16 | async-start | bytes 1310720
  1422.2 320.8 %all-reduce.29.cloned.1.call-start = ((), (), s32[]{:S(2)}) async-start(), calls=%async_computation.8 | async-start | bytes 655360 | tf_op jit(solution)/shard_map/psum | solution.py:103
  1424.7 191.2 %copy-start.3 = (bf16[2,64,640]{2,1,0:T(8,128)(2,1)S(1)}, bf16[2,64,640]{2,1,0:T(8,128)(2,1)}, u32[]{:S(2)}) copy-start(bf16[2,64,640]{2,1,0:T(8,128)(2,1)} %all-reduce.27.cloned.1.call-done) | copy-start | bytes 491524
  1615.9 127.1 %copy-start.7 = (bf16[4,2,64,128]{3,2,1,0:T(8,128)(2,1)S(1)}, bf16[4,2,64,128]{3,2,1,0:T(8,128)(2,1)}, u32[]{:S(2)}) copy-start(bf16[4,2,64,128]{3,2,1,0:T(8,128)(2,1)} %reshape.190) | copy-start | bytes 393220
  1615.9 346.7 %reduce-scatter.7.cloned.1.call-start = ((), (), s32[]{:S(2)}) async-start(), calls=%async_computation.9 | async-start | bytes 1351680 | tf_op jit(solution)/shard_map/reduce_scatter | solution.py:89
  1616.5 128.0 %copy-start.6 = (bf16[8,64,128]{2,1,0:T(8,128)(2,1)S(1)}, bf16[8,64,128]{2,1,0:T(8,128)(2,1)}, u32[]{:S(2)}) copy-start(bf16[8,64,128]{2,1,0:T(8,128)(2,1)} %reshape.213) | copy-start | bytes 393220
  1747.1 300.0 %copy-start.9 = (bf16[15,64,128]{2,1,0:T(8,128)(2,1)S(1)}, bf16[15,64,128]{2,1,0:T(8,128)(2,1)}, u32[]{:S(2)}) copy-start(bf16[15,64,128]{2,1,0:T(8,128)(2,1)} %param.13) | copy-start | bytes 737284
  1747.1 299.9 %all-gather.2.cloned.1.call-start = ((), (), s32[]{:S(2)}) async-start(), calls=%async_computation.10 | async-start | bytes 1351680 | tf_op jit(solution)/shard_map/all_gather | solution.py:94
  1964.1 204.8 %all-reduce.31.cloned.1.call-start = ((), (), s32[]{:S(2)}) async-start(), calls=%async_computation.11 | async-start | bytes 1310720 | tf_op jit(solution)/shard_map/psum | solution.py:103
  (6 other events, 72.2 us)
Sparse Core Ops, SparseCore 0:
  38.3 153.5 all-reduce.16
  195.5 59.0 reduce-scatter.8
  276.3 152.1 all-reduce.18
  431.2 115.4 all-reduce.32
  564.2 150.9 all-reduce.20
  717.4 109.0 all-reduce.34
  844.4 147.5 all-reduce.22
  994.5 109.0 all-reduce.24
  1107.0 150.7 all-reduce.36
  1296.8 122.3 all-reduce.26
  1422.6 153.4 all-reduce.38
  1616.0 126.9 all-reduce.28
  1747.4 215.1 reduce-scatter.6
  1965.6 81.3 all-gather.1
  2050.0 118.8 all-reduce.30
where the time goes:
time: 2180 us
  waiting for transfers between devices  1950 us (89%)
  blocking collectives  152 us (7%)
  local copies, waits for them, and re-layouts  24.5 us (1%)
  matrix products  24.4 us (1%)
    psum x4, waiting for transfers between devices, solve_all(): forward.append(lax.psum(partial_value.astype(jnp.bfloat16), 'pcol'))  599 us
    unnamed x20, waiting for transfers between devices  582 us
    psum x4, waiting for transfers between devices, solve_all(): backward[height] = lax.psum(partial_value.astype(jnp.bfloat16), 'prow')  475 us
    reduce_scatter x1, waiting for transfers between devices, solve_all(): lax.psum_scatter(partial_value.astype(jnp.bfloat16), 'pcol', scatter_dime...  215 us
    all_gather x1, waiting for transfers between devices, solve_all(): residual = lax.all_gather(residual_share, 'pcol', axis=2, tiled=True)  82.9 us
    all_gather x4, blocking collectives, solve_all(): residual = lax.all_gather(residual_share, 'prow', axis=2, tiled=True)  79.2 us
    all_gather x2, blocking collectives, solve_all(): residual = lax.all_gather(residual_share, 'pcol', axis=2, tiled=True)  72.7 us
  transfers between devices with their start and end apart: 15, of which 15 were waited for; matrix products, arithmetic and copies ran while one was open for 1% of the time, Pallas kernels for 0%

commit v1 on v0

v1 whole, which is shorter than its diff:
```python
import jax
import jax.numpy as jnp
from jax import lax
from jax.sharding import Mesh, PartitionSpec as P

BF = jnp.bfloat16
F32 = jnp.float32
PROW = ("z", "core")
Y = ("y2", "y1", "y0")
YHIGH = ("y2", "y1")
GROUP = ("x", "y0")


def swap(blocks, axes):
    return lax.all_to_all(blocks, axes, 0, 0, tiled=True)


def share(block, axes, count):
    return swap(jnp.broadcast_to(block[None], (count,) + block.shape), axes)


def masked(panels, pattern):
    lane = lax.broadcasted_iota(jnp.int32, (1, 1, panels.shape[2]), 2)
    keep = jnp.where(lane < panels.shape[2] // 2, pattern[:, :, 0:1], pattern[:, :, 1:2])
    return jnp.where(keep > 0, panels, jnp.zeros((), panels.dtype))


def spread_leaf(tiles):
    return jnp.swapaxes(swap(jnp.stack(tiles, axis=1), Y), 0, 1)


def spread_upper(tiles):
    wide = [jnp.repeat(t, 4 // t.shape[0], axis=0) for t in tiles]
    return jnp.swapaxes(swap(jnp.stack(wide, axis=1), YHIGH), 0, 1)


def gather(parts):
    flat = jnp.concatenate([p.reshape((-1,) + p.shape[2:]) for p in parts], axis=0)
    full = lax.all_gather(flat, PROW, axis=0, tiled=False)
    out, at = [], 0
    for p in parts:
        got = []
        for _ in range(p.shape[0]):
            got.append(full[:, at : at + p.shape[1]])
            at += p.shape[1]
        out.append(got)
    return out


def by_rows(panel, vector):
    return jnp.einsum("pnc,psrc->snr", vector, panel, preferred_element_type=F32)


def by_cols(panel, vector):
    return jnp.einsum("snr,psrc->pnc", vector, panel, preferred_element_type=F32)


def sum_x(part):
    return share(part.astype(BF), "x", 4).astype(F32).reshape((4,) + part.shape).sum(0)


def scatter_group(part):
    pieces = swap(part.astype(BF).reshape(8, 2, *part.shape[1:]), GROUP)
    return pieces.astype(F32).sum(0)


def gather_group(own):
    return share(own, GROUP, 8).reshape((16,) + own.shape[1:])


def local(right_side, lower_panels, lower_pattern, upper_panels, upper_pattern, lower_inverse, upper_inverse):
    y0 = lax.axis_index("y0")
    y1 = lax.axis_index("y1")
    yi = lax.axis_index(Y)
    gi = lax.axis_index(GROUP)

    low = masked(lower_panels, lower_pattern)
    up = masked(upper_panels, upper_pattern)
    li, ui = lower_inverse, upper_inverse

    rhs = jnp.swapaxes(right_side, 1, 2)
    nodes = jnp.stack(
        [rhs[0:8], jnp.repeat(rhs[8:12], 2, 0), jnp.repeat(rhs[12:14], 4, 0), jnp.repeat(rhs[14:15], 8, 0)], axis=1
    )
    nodes = swap(nodes, Y)
    b0 = nodes[:, 0]
    n = b0.shape[1]
    upper_b = nodes[:, 1:].reshape(4, 2, 3, n, 64)
    upper_b = jnp.where(y0 == 0, upper_b[:, 0], upper_b[:, 1]).astype(F32)

    (p_li0, p_l01), = gather([spread_leaf([li[0:8], low[0:8]])])
    upper_fwd = spread_upper([li[8:12], low[24:28], low[28:32], li[12:14], low[32:34], li[14:15]])
    leaf_fwd = spread_leaf([low[8:16], low[16:24]])
    (p_l02, p_l03), (p_li1, p_l12, p_l13, p_li2, p_l23, p_li3) = gather([leaf_fwd, upper_fwd])
    upper_bwd = spread_upper([ui[14:15], up[32:34], ui[12:14], up[24:28], up[28:32], ui[8:12]])
    leaf_bwd = spread_leaf([up[0:8], up[8:16], up[16:24], ui[0:8]])
    (p_ui3, p_u23, p_ui2, p_u12, p_u13, p_ui1), (p_u01, p_u02, p_u03, p_ui0) = gather([upper_bwd, leaf_bwd])

    def parity(blocks):
        return jnp.swapaxes(blocks.reshape((4, 2) + blocks.shape[1:]), 0, 1)

    mine = (lax.broadcasted_iota(jnp.int32, (2, 1, 1, 1), 0) == y0)

    def add_mine(blocks, extra):
        return blocks + jnp.where(mine, extra[None], 0.0)

    v0 = sum_x(by_cols(p_li0, b0)).astype(BF)
    part = parity(by_rows(p_l01, v0)).astype(BF)
    update = swap(part, "y0").astype(F32).sum(0)
    res = (upper_b[:, 0] - update).astype(BF)

    own1 = scatter_group(by_cols(p_li1, res)).astype(BF)
    v1 = gather_group(own1)
    part = add_mine(parity(by_rows(p_l02, v0)), by_rows(p_l12, v1)).astype(BF)
    part = jnp.broadcast_to(part[None], (2,) + part.shape).reshape((4,) + part.shape[1:])
    update = swap(part, ("y1", "y0")).astype(F32).sum(0)
    res = (upper_b[:, 1] - update).astype(BF)

    own2 = scatter_group(by_cols(p_li2, res)).astype(BF)
    v2 = gather_group(own2)
    top = by_rows(p_l13, v1) + jnp.where(y1 == 0, by_rows(p_l23, v2), 0.0)
    part = add_mine(parity(by_rows(p_l03, v0)), top).astype(BF)
    part = jnp.broadcast_to(part[None], (4,) + part.shape).reshape((8,) + part.shape[1:])
    update = swap(part, Y).astype(F32).sum(0)
    res = (upper_b[:, 2] - update).astype(BF)

    v3 = gather_group(scatter_group(by_cols(p_li3, res)).astype(BF))

    s3 = by_rows(p_ui3, v3).astype(BF)
    own = own2.astype(F32) - scatter_group(by_cols(p_u23, s3))
    s2 = by_rows(p_ui2, gather_group(own.astype(BF))).astype(BF)
    own = own1.astype(F32) - scatter_group(by_cols(p_u12, s2) + by_cols(p_u13, s3))
    s1 = by_rows(p_ui1, gather_group(own.astype(BF))).astype(BF)

    uppers = share(jnp.stack([s1, s2, s3]), "y0", 2).reshape(2, 3, 4, n, 64)
    uppers = jnp.transpose(uppers, (1, 2, 0, 3, 4)).reshape(3, 8, n, 64)
    part = by_cols(p_u01, uppers[0]) + by_cols(p_u02, uppers[1]) + by_cols(p_u03, uppers[2])
    res = (v0.astype(F32) - sum_x(part)).astype(BF)
    s0 = by_rows(p_ui0, res).astype(BF)

    got = swap(jnp.stack([s0, uppers[0], uppers[1]], axis=1), Y)
    last = lax.dynamic_index_in_dim(uppers[2], yi, 0, keepdims=True)
    out = jnp.concatenate([got[:, 0], got[0::2, 1], got[0::4, 2], last], axis=0)
    return jnp.swapaxes(out, 1, 2)


def solution(mesh):
    fine = Mesh(mesh.devices.reshape(8, 2, 4, 2, 2, 2), ("z", "core", "x", "y2", "y1", "y0"))
    spec = P(None, ("x", "y2", "y1", "y0"), ("z", "core"))
    return jax.shard_map(local, mesh=fine, in_specs=(spec,) * 7, out_specs=spec, check_vma=False)
```

time: 2180 us -> 342 us (0.16)
  the two profiles are of different devices: /device:TPU:1 before, /device:TPU:2 now
where the time goes in v1:
time: 342 us; the launch traced here: 339 us
  blocking collectives  119 us (35%)
  waiting for transfers between devices  89.6 us (26%)
  starting transfers between devices  51.3 us (15%)
  matrix products  40.9 us (12%)
  local copies, waits for them, and re-layouts  19.1 us (6%)
  between operations  13.8 us (4%)
  other arithmetic  5.08 us (1%)
    all_to_all x11, blocking collectives, swap(): return lax.all_to_all(blocks, axes, 0, 0, tiled=True)  119 us
    all_to_all x12, waiting for transfers between devices, swap(): return lax.all_to_all(blocks, axes, 0, 0, tiled=True)  79.9 us
    all_to_all x12, starting transfers between devices, swap(): return lax.all_to_all(blocks, axes, 0, 0, tiled=True)  51.3 us
    dot_general x10, matrix products, by_rows(): jnp.einsum('pnc,psrc->snr', vector, panel, preferred_element_type=F32)  21.8 us
    dot_general x10, matrix products, by_cols(): jnp.einsum('snr,psrc->pnc', vector, panel, preferred_element_type=F32)  19.1 us
    all_gather x3, waiting for transfers between devices, gather(): full = lax.all_gather(flat, PROW, axis=0, tiled=False)  9.61 us
    unnamed x26, local copies, waits for them, and re-layouts  7.65 us
  transfers between devices with their start and end apart: 15, of which 13 were waited for; matrix products, arithmetic and copies ran while one was open for 12% of the time, Pallas kernels for 0%

profile of v1, /device:TPU:2, one launch (start us, length us, event | category | flops | bytes accessed | tf_op | source)
XLA Modules:
  0.0 339.2 jit_solution(12890388642014071213)
XLA Ops:
  10.6 18.8 %all_to_all.115 = bf16[8,2,64,128]{3,2,1,0:T(8,128)(2,1)S(1)} all-to-all(bf16[8,2,64,128]{3,2,1,0:T(8,128)(2,1)S(1)} %copy.113), channel_id=1, replica_groups=mesh['z'=8,'core'=2,'x'=4,'y2'=2,'y1'=2,'y0'=2] {'y2','y1','y0'}, dimensions={0} | all-to-all | bytes 524288 | tf_op jit(solution)/shard_map/all_to_all | solution.py:15
  37.5 7.2 %all-to-all-done.5 = bf16[8,2,64,128]{3,2,1,0:T(8,128)(2,1)S(1)} async-done(((bf16[8,2,64,128]{3,2,1,0:T(8,128)(2,1)}), bf16[8,2,64,128]{3,2,1,0:T(8,128)(2,1)S(1)}, u32[]{:S(2)}, u32[]{:S(2)}) %all-to-all-start.5) | async-done | bytes 262176 | tf_op jit(solution)/shard_map/all_to_all | solution.py:15
  48.2 11.5 %all-to-all-done.6 = bf16[4,6,64,128]{3,2,1,0:T(8,128)(2,1)S(1)} async-done(((bf16[4,6,64,128]{3,2,1,0:T(8,128)(2,1)}), bf16[4,6,64,128]{3,2,1,0:T(8,128)(2,1)S(1)}, u32[]{:S(2)}, u32[]{:S(2)}) %all-to-all-start.6) | async-done | bytes 393248 | tf_op jit(solution)/shard_map/all_to_all | solution.py:15
  69.0 8.8 %all-to-all-done = bf16[4,6,64,128]{3,2,1,0:T(8,128)(2,1)S(1)} async-done(((bf16[4,6,64,128]{3,2,1,0:T(8,128)(2,1)}), bf16[4,6,64,128]{3,2,1,0:T(8,128)(2,1)S(1)}, u32[]{:S(2)}, u32[]{:S(2)}) %all-to-all-start) | async-done | bytes 393248 | tf_op jit(solution)/shard_map/all_to_all | solution.py:15
  82.0 13.2 %all-to-all-done.1 = bf16[8,4,64,128]{3,2,1,0:T(8,128)(2,1)S(1)} async-done(((bf16[8,4,64,128]{3,2,1,0:T(8,128)(2,1)}), bf16[8,4,64,128]{3,2,1,0:T(8,128)(2,1)S(1)}, u32[]{:S(2)}, u32[]{:S(2)}) %all-to-all-start.1) | async-done | bytes 524320 | tf_op jit(solution)/shard_map/all_to_all | solution.py:15
  96.8 11.8 %all_to_all.116 = bf16[8,2,5120]{2,1,0:T(2,128)(2,1)S(1)} all-to-all(bf16[8,2,5120]{2,1,0:T(2,128)(2,1)S(1)} %reshape.261), channel_id=1, replica_groups=mesh['z'=8,'core'=2,'x'=4,'y2'=2,'y1'=2,'y0'=2] {'y2','y1','y0'}, dimensions={0} | all-to-all | bytes 327680 | tf_op jit(solution)/shard_map/all_to_all | solution.py:15
  116.9 7.3 %all-to-all-done.4 = bf16[4,16,40,128]{3,2,1,0:T(8,128)(2,1)S(1)} async-done(((bf16[4,16,40,128]{3,2,1,0:T(8,128)(2,1)}), bf16[4,16,40,128]{3,2,1,0:T(8,128)(2,1)S(1)}, u32[]{:S(2)}, u32[]{:S(2)}) %all-to-all-start.4) | async-done | bytes 655392 | tf_op jit(solution)/shard_map/all_to_all | solution.py:15
  135.1 9.6 %all-gather.10.cloned.1.call-done = bf16[640,64,128]{2,1,0:T(8,128)(2,1)} async-done(((bf16[40,64,128]{2,1,0:T(8,128)(2,1)}), bf16[640,64,128]{2,1,0:T(8,128)(2,1)}) %all-gather.10.cloned.1.call-update) | async-done | bytes 10485776 | tf_op jit(solution)/shard_map/all_gather | solution.py:39
  147.0 5.7 %all-to-all-start.8 = ((bf16[8,2,40,128]{3,2,1,0:T(8,128)(2,1)}), bf16[8,2,40,128]{3,2,1,0:T(8,128)(2,1)S(1)}, u32[]{:S(2)}, u32[]{:S(2)}) async-start(bf16[8,2,40,128]{3,2,1,0:T(8,128)(2,1)} %bitcast.60), calls=%async_computation.8 | async-start | bytes 327680 | tf_op jit(solution)/shard_map/all_to_all | solution.py:15
  152.7 5.1 %all-to-all-done.8 = bf16[8,2,40,128]{3,2,1,0:T(8,128)(2,1)S(1)} async-done(((bf16[8,2,40,128]{3,2,1,0:T(8,128)(2,1)}), bf16[8,2,40,128]{3,2,1,0:T(8,128)(2,1)S(1)}, u32[]{:S(2)}, u32[]{:S(2)}) %all-to-all-start.8) | async-done | bytes 163872 | tf_op jit(solution)/shard_map/all_to_all | solution.py:15
  158.6 5.0 %all-to-all-start.9 = ((bf16[8,2,40,128]{3,2,1,0:T(8,128)(2,1)}), bf16[8,2,40,128]{3,2,1,0:T(8,128)(2,1)S(1)}, u32[]{:S(2)}, u32[]{:S(2)}) async-start(bf16[8,2,40,128]{3,2,1,0:T(8,128)(2,1)} %broadcast_in_dim.225), calls=%async_computation.9 | async-start | bytes 327680 | tf_op jit(solution)/shard_map/all_to_all | solution.py:15
  170.9 9.6 %all_to_all.117 = bf16[4,2,5120]{2,1,0:T(2,128)(2,1)S(1)} all-to-all(bf16[4,2,5120]{2,1,0:T(2,128)(2,1)S(1)} %reshape.265), channel_id=1, replica_groups=mesh['z'=8,'core'=2,'x'=4,'y2'=2,'y1'=2,'y0'=2] {'y1','y0'}, dimensions={0} | all-to-all | bytes 163840 | tf_op jit(solution)/shard_map/all_to_all | solution.py:15
  187.7 5.2 %all-to-all-done.11 = bf16[8,2,40,128]{3,2,1,0:T(8,128)(2,1)S(1)} async-done(((bf16[8,2,40,128]{3,2,1,0:T(8,128)(2,1)}), bf16[8,2,40,128]{3,2,1,0:T(8,128)(2,1)S(1)}, u32[]{:S(2)}, u32[]{:S(2)}) %all-to-all-start.11) | async-done | bytes 163872 | tf_op jit(solution)/shard_map/all_to_all | solution.py:15
  193.6 5.0 %all-to-all-start.12 = ((bf16[8,2,40,128]{3,2,1,0:T(8,128)(2,1)}), bf16[8,2,40,128]{3,2,1,0:T(8,128)(2,1)S(1)}, u32[]{:S(2)}, u32[]{:S(2)}) async-start(bf16[8,2,40,128]{3,2,1,0:T(8,128)(2,1)} %broadcast_in_dim.229), calls=%async_computation.12 | async-start | bytes 327680 | tf_op jit(solution)/shard_map/all_to_all | solution.py:15
  207.9 13.7 %all_to_all.118 = bf16[8,2,5120]{2,1,0:T(2,128)(2,1)S(1)} all-to-all(bf16[8,2,5120]{2,1,0:T(2,128)(2,1)S(1)} %reshape.267), channel_id=1, replica_groups=mesh['z'=8,'core'=2,'x'=4,'y2'=2,'y1'=2,'y0'=2] {'y2','y1','y0'}, dimensions={0} | all-to-all | bytes 327680 | tf_op jit(solution)/shard_map/all_to_all | solution.py:15
  223.5 9.4 %all_to_all.119 = bf16[8,2,40,128]{3,2,1,0:T(8,128)(2,1)S(1)} all-to-all(bf16[8,2,40,128]{3,2,1,0:T(8,128)(2,1)S(1)} %bitcast.417), channel_id=1, replica_groups=mesh['z'=8,'core'=2,'x'=4,'y2'=2,'y1'=2,'y0'=2] {'x','y0'}, dimensions={0} | all-to-all | bytes 327680 | tf_op jit(solution)/shard_map/all_to_all | solution.py:15
  233.0 9.8 %all_to_all.120 = bf16[8,2,40,128]{3,2,1,0:T(8,128)(2,1)S(1)} all-to-all(bf16[8,2,40,128]{3,2,1,0:T(8,128)(2,1)S(1)} %broadcast_in_dim.233), channel_id=1, replica_groups=mesh['z'=8,'core'=2,'x'=4,'y2'=2,'y1'=2,'y0'=2] {'x','y0'}, dimensions={0} | all-to-all | bytes 327680 | tf_op jit(solution)/shard_map/all_to_all | solution.py:15
  246.2 9.3 %all_to_all.121 = bf16[8,2,40,128]{3,2,1,0:T(8,128)(2,1)S(1)} all-to-all(bf16[8,2,40,128]{3,2,1,0:T(8,128)(2,1)S(1)} %bitcast.419), channel_id=1, replica_groups=mesh['z'=8,'core'=2,'x'=4,'y2'=2,'y1'=2,'y0'=2] {'x','y0'}, dimensions={0} | all-to-all | bytes 327680 | tf_op jit(solution)/shard_map/all_to_all | solution.py:15
  256.3 5.0 %all-to-all-start.17 = ((bf16[8,2,40,128]{3,2,1,0:T(8,128)(2,1)}), bf16[8,2,40,128]{3,2,1,0:T(8,128)(2,1)S(1)}, u32[]{:S(2)}, u32[]{:S(2)}) async-start(bf16[8,2,40,128]{3,2,1,0:T(8,128)(2,1)} %broadcast_in_dim.234), calls=%async_computation.17 | async-start | bytes 327680 | tf_op jit(solution)/shard_map/all_to_all | solution.py:15
  269.9 9.4 %all_to_all.122 = bf16[8,2,40,128]{3,2,1,0:T(8,128)(2,1)S(1)} all-to-all(bf16[8,2,40,128]{3,2,1,0:T(8,128)(2,1)S(1)} %bitcast.418), channel_id=1, replica_groups=mesh['z'=8,'core'=2,'x'=4,'y2'=2,'y1'=2,'y0'=2] {'x','y0'}, dimensions={0} | all-to-all | bytes 327680 | tf_op jit(solution)/shard_map/all_to_all | solution.py:15
  279.4 9.3 %all_to_all.123 = bf16[8,2,40,128]{3,2,1,0:T(8,128)(2,1)S(1)} all-to-all(bf16[8,2,40,128]{3,2,1,0:T(8,128)(2,1)S(1)} %broadcast_in_dim.235), channel_id=1, replica_groups=mesh['z'=8,'core'=2,'x'=4,'y2'=2,'y1'=2,'y0'=2] {'x','y0'}, dimensions={0} | all-to-all | bytes 327680 | tf_op jit(solution)/shard_map/all_to_all | solution.py:15
  290.8 6.8 %all_to_all.124 = bf16[2,2,15360]{2,1,0:T(2,128)(2,1)S(1)} all-to-all(bf16[2,2,15360]{2,1,0:T(2,128)(2,1)S(1)} %reshape.269), channel_id=1, replica_groups=mesh['z'=8,'core'=2,'x'=4,'y2'=2,'y1'=2,'y0'=2] {'y0'}, dimensions={0} | all-to-all | bytes 245760 | tf_op jit(solution)/shard_map/all_to_all | solution.py:15
  304.3 11.4 %all_to_all.125 = bf16[4,16,40,128]{3,2,1,0:T(8,128)(2,1)S(1)} all-to-all(bf16[4,16,40,128]{3,2,1,0:T(8,128)(2,1)S(1)} %broadcast_in_dim.237), channel_id=1, replica_groups=mesh['z'=8,'core'=2,'x'=4,'y2'=2,'y1'=2,'y0'=2] {'x'}, dimensions={0} | all-to-all | bytes 1310720 | tf_op jit(solution)/shard_map/all_to_all | solution.py:15
  322.8 8.9 %all-to-all-done.22 = bf16[8,2,3840]{2,1,0:T(2,128)(2,1)S(1)} async-done(((bf16[8,2,3840]{2,1,0:T(2,128)(2,1)}), bf16[8,2,3840]{2,1,0:T(2,128)(2,1)S(1)}, u32[]{:S(2)}, u32[]{:S(2)}) %all-to-all-start.22) | async-done | bytes 122912 | tf_op jit(solution)/shard_map/all_to_all | solution.py:15
  (153 shorter events, 108.6 us)
Async XLA Ops:
  6.5 54.1 %copy-start = (bf16[15,64,128]{2,1,0:T(8,128)(2,1)S(1)}, bf16[15,64,128]{2,1,0:T(8,128)(2,1)}, u32[]{:S(2)}) copy-start(bf16[15,64,128]{2,1,0:T(8,128)(2,1)} %param.13) | copy-start | bytes 737284
  6.5 55.4 %slice-start = ((bf16[15,64,128]{2,1,0:T(8,128)(2,1)}), bf16[2,64,128]{2,1,0:T(8,128)(2,1)S(1)}, s32[]{:S(2)}) async-start(bf16[15,64,128]{2,1,0:T(8,128)(2,1)} %param.13), calls=%async_computation.26 | async-start | bytes 65536 | tf_op jit(solution)/shard_map/slice | solution.py:95
  6.5 102.4 %all-gather.6.cloned.1.call-start = ((), (), s32[]{:S(2)}) async-start(), calls=%async_computation.23 | async-start | bytes 4456448 | tf_op jit(solution)/shard_map/all_gather | solution.py:39
  9.5 86.8 %copy-start.1 = (bf16[15,64,40]{1,2,0:T(8,128)(2,1)S(1)}, bf16[15,64,40]{1,2,0:T(8,128)(2,1)}, u32[]{:S(2)}) copy-start(bf16[15,64,40]{1,2,0:T(8,128)(2,1)} %param.7) | copy-start | bytes 230404
  30.8 13.8 %all-to-all-start.5 = ((bf16[8,2,64,128]{3,2,1,0:T(8,128)(2,1)}), bf16[8,2,64,128]{3,2,1,0:T(8,128)(2,1)S(1)}, u32[]{:S(2)}, u32[]{:S(2)}) async-start(bf16[8,2,64,128]{3,2,1,0:T(8,128)(2,1)} %copy.117), calls=%async_computation.5 | async-start | bytes 524288 | tf_op jit(solution)/shard_map/all_to_all | solution.py:15
  44.7 15.0 %all-to-all-start.6 = ((bf16[4,6,64,128]{3,2,1,0:T(8,128)(2,1)}), bf16[4,6,64,128]{3,2,1,0:T(8,128)(2,1)S(1)}, u32[]{:S(2)}, u32[]{:S(2)}) async-start(bf16[4,6,64,128]{3,2,1,0:T(8,128)(2,1)} %copy.119), calls=%async_computation.6 | async-start | bytes 786432 | tf_op jit(solution)/shard_map/all_to_all | solution.py:15
  48.1 96.6 %all-gather.10.cloned.1.call-start = ((), (), s32[]{:S(2)}) async-start(), calls=%async_computation.25 | async-start | bytes 11141120 | tf_op jit(solution)/shard_map/all_gather | solution.py:39
  64.6 13.3 %all-to-all-start = ((bf16[4,6,64,128]{3,2,1,0:T(8,128)(2,1)}), bf16[4,6,64,128]{3,2,1,0:T(8,128)(2,1)S(1)}, u32[]{:S(2)}, u32[]{:S(2)}) async-start(bf16[4,6,64,128]{3,2,1,0:T(8,128)(2,1)} %bitcast_dynamic-update-slice_fusion.1), calls=%async_computation | async-start | bytes 786432 | tf_op jit(solution)/shard_map/all_to_all | solution.py:15
  77.9 17.3 %all-to-all-start.1 = ((bf16[8,4,64,128]{3,2,1,0:T(8,128)(2,1)}), bf16[8,4,64,128]{3,2,1,0:T(8,128)(2,1)S(1)}, u32[]{:S(2)}, u32[]{:S(2)}) async-start(bf16[8,4,64,128]{3,2,1,0:T(8,128)(2,1)} %copy.110), calls=%async_computation.1 | async-start | bytes 1048576 | tf_op jit(solution)/shard_map/all_to_all | solution.py:15
  81.9 160.9 %all-gather.8.cloned.1.call-start = ((), (), s32[]{:S(2)}) async-start(), calls=%async_computation.24 | async-start | bytes 15597568 | tf_op jit(solution)/shard_map/all_gather | solution.py:39
  112.0 12.2 %all-to-all-start.4 = ((bf16[4,16,40,128]{3,2,1,0:T(8,128)(2,1)}), bf16[4,16,40,128]{3,2,1,0:T(8,128)(2,1)S(1)}, u32[]{:S(2)}, u32[]{:S(2)}) async-start(bf16[4,16,40,128]{3,2,1,0:T(8,128)(2,1)} %broadcast_in_dim.218), calls=%async_computation.4 | async-start | bytes 1310720 | tf_op jit(solution)/shard_map/all_to_all | solution.py:15
  127.7 7.3 %all-to-all-start.7 = ((bf16[2,2,5120]{2,1,0:T(2,128)(2,1)}), bf16[2,2,5120]{2,1,0:T(2,128)(2,1)S(1)}, u32[]{:S(2)}, u32[]{:S(2)}) async-start(bf16[2,2,5120]{2,1,0:T(2,128)(2,1)} %reshape.263), calls=%async_computation.7 | async-start | bytes 81920 | tf_op jit(solution)/shard_map/all_to_all | solution.py:15
  147.0 10.9 %all-to-all-start.8 = ((bf16[8,2,40,128]{3,2,1,0:T(8,128)(2,1)}), bf16[8,2,40,128]{3,2,1,0:T(8,128)(2,1)S(1)}, u32[]{:S(2)}, u32[]{:S(2)}) async-start(bf16[8,2,40,128]{3,2,1,0:T(8,128)(2,1)} %bitcast.60), calls=%async_computation.8 | async-start | bytes 327680 | tf_op jit(solution)/shard_map/all_to_all | solution.py:15
  158.6 10.2 %all-to-all-start.9 = ((bf16[8,2,40,128]{3,2,1,0:T(8,128)(2,1)}), bf16[8,2,40,128]{3,2,1,0:T(8,128)(2,1)S(1)}, u32[]{:S(2)}, u32[]{:S(2)}) async-start(bf16[8,2,40,128]{3,2,1,0:T(8,128)(2,1)} %broadcast_in_dim.225), calls=%async_computation.9 | async-start | bytes 327680 | tf_op jit(solution)/shard_map/all_to_all | solution.py:15
  183.0 10.0 %all-to-all-start.11 = ((bf16[8,2,40,128]{3,2,1,0:T(8,128)(2,1)}), bf16[8,2,40,128]{3,2,1,0:T(8,128)(2,1)S(1)}, u32[]{:S(2)}, u32[]{:S(2)}) async-start(bf16[8,2,40,128]{3,2,1,0:T(8,128)(2,1)} %bitcast.78), calls=%async_computation.11 | async-start | bytes 327680 | tf_op jit(solution)/shard_map/all_to_all | solution.py:15
  193.6 10.1 %all-to-all-start.12 = ((bf16[8,2,40,128]{3,2,1,0:T(8,128)(2,1)}), bf16[8,2,40,128]{3,2,1,0:T(8,128)(2,1)S(1)}, u32[]{:S(2)}, u32[]{:S(2)}) async-start(bf16[8,2,40,128]{3,2,1,0:T(8,128)(2,1)} %broadcast_in_dim.229), calls=%async_computation.12 | async-start | bytes 327680 | tf_op jit(solution)/shard_map/all_to_all | solution.py:15
  256.3 10.3 %all-to-all-start.17 = ((bf16[8,2,40,128]{3,2,1,0:T(8,128)(2,1)}), bf16[8,2,40,128]{3,2,1,0:T(8,128)(2,1)S(1)}, u32[]{:S(2)}, u32[]{:S(2)}) async-start(bf16[8,2,40,128]{3,2,1,0:T(8,128)(2,1)} %broadcast_in_dim.234), calls=%async_computation.17 | async-start | bytes 327680 | tf_op jit(solution)/shard_map/all_to_all | solution.py:15
  319.4 12.3 %all-to-all-start.22 = ((bf16[8,2,3840]{2,1,0:T(2,128)(2,1)}), bf16[8,2,3840]{2,1,0:T(2,128)(2,1)S(1)}, u32[]{:S(2)}, u32[]{:S(2)}) async-start(bf16[8,2,3840]{2,1,0:T(2,128)(2,1)} %reshape.271), calls=%async_computation.22 | async-start | bytes 245760 | tf_op jit(solution)/shard_map/all_to_all | solution.py:15
Sparse Core Ops, SparseCore 0:
  30.2 45.0 all-gather.5
  77.4 67.2 all-gather.9
  146.9 86.9 all-gather.7

commit v2 on v1

v2 whole, which is shorter than its diff:
```python
import jax
import jax.numpy as jnp
from jax import lax
from jax.sharding import Mesh, PartitionSpec as P

BF = jnp.bfloat16
F32 = jnp.float32
PROW = ("z", "core")
Y = ("y2", "y1", "y0")
YHIGH = ("y2", "y1")


def swap(blocks, axes):
    return lax.all_to_all(blocks, axes, 0, 0, tiled=True)


def share(block, axes, count):
    return swap(jnp.broadcast_to(block[None], (count,) + block.shape), axes)


def masked(panels, pattern):
    lane = lax.broadcasted_iota(jnp.int32, (1, 1, panels.shape[2]), 2)
    keep = jnp.where(lane < panels.shape[2] // 2, pattern[:, :, 0:1], pattern[:, :, 1:2])
    return jnp.where(keep > 0, panels, jnp.zeros((), panels.dtype))


def spread_leaf(tiles):
    return jnp.swapaxes(swap(jnp.stack(tiles, axis=1), Y), 0, 1)


def spread_upper(tiles):
    wide = [jnp.repeat(t, 4 // t.shape[0], axis=0) for t in tiles]
    return jnp.swapaxes(swap(jnp.stack(wide, axis=1), YHIGH), 0, 1)


def gather(parts, groups=None):
    flat = jnp.concatenate([p.reshape((-1,) + p.shape[2:]) for p in parts], axis=0)
    full = lax.all_gather(flat, PROW, axis=0, tiled=False)
    out, at = [], 0
    for p, sizes in zip(parts, groups):
        got = []
        for size in sizes:
            got.append(full[:, at : at + size * p.shape[1]])
            at += size * p.shape[1]
        out.append(got)
    return out


def collect(part, axis):
    return lax.all_gather(part, axis, axis=0, tiled=False).astype(F32).sum(0)


def by_rows(panel, vector):
    return jnp.einsum("pnc,psrc->snr", vector, panel, preferred_element_type=F32)


def by_cols(panel, vector):
    return jnp.einsum("snr,psrc->pnc", vector, panel, preferred_element_type=F32)


def sum_x(part):
    return share(part.astype(BF), "x", 4).astype(F32).reshape((4,) + part.shape).sum(0)


def local(right_side, lower_panels, lower_pattern, upper_panels, upper_pattern, lower_inverse, upper_inverse):
    y0 = lax.axis_index("y0")
    yi = lax.axis_index(Y)

    li, ui = lower_inverse, upper_inverse
    head = masked(lower_panels[0:8], lower_pattern[0:8])

    def parity(blocks):
        pairs = blocks.reshape(blocks.shape[:-3] + (4, 2) + blocks.shape[-2:])
        return jnp.where(y0 == 0, pairs[..., 0, :, :], pairs[..., 1, :, :])

    first = spread_leaf([li[0:8], head, jnp.repeat(li[8:12], 2, 0)])
    (p_li0, p_l01), (p_li1,) = gather([first[0:2], parity(first[2:3])], ((1, 1), (1,)))

    right_side, lower_panels, lower_pattern, li, first = lax.optimization_barrier(
        (right_side, lower_panels, lower_pattern, li, first)
    )
    low = masked(lower_panels, lower_pattern)
    rhs = jnp.swapaxes(right_side, 1, 2)
    nodes = jnp.stack(
        [rhs[0:8], jnp.repeat(rhs[8:12], 2, 0), jnp.repeat(rhs[12:14], 4, 0), jnp.repeat(rhs[14:15], 8, 0)], axis=1
    )
    nodes = swap(nodes, Y)
    b0 = nodes[:, 0]
    n = b0.shape[1]
    b1, b2, b3 = (nodes[:, k].astype(F32) for k in (1, 2, 3))

    leaf_fwd = spread_leaf([low[8:16], low[16:24], jnp.repeat(li[12:14], 4, 0), jnp.repeat(li[14:15], 8, 0)])
    upper_fwd = spread_upper([low[24:28], low[28:32], low[32:34]])
    p_leaf, p_upper = gather([leaf_fwd, upper_fwd], ((2, 1, 1), (2, 1)))
    (p_l0, p_li2, p_li3), (p_l1, p_l23) = p_leaf, p_upper

    mine = lax.broadcasted_iota(jnp.int32, (1, 1, 2, 1, 1), 2) == y0

    nothing = (leaf_fwd[0, 0, 0, 0] + upper_fwd[0, 0, 0, 0]) * jnp.zeros((), BF)
    part = by_cols(p_li0, b0 + nothing).astype(BF)
    part, upper_panels, upper_pattern, ui = lax.optimization_barrier((part, upper_panels, upper_pattern, ui))
    up = masked(upper_panels, upper_pattern)
    upper_bwd = spread_upper([ui[14:15], up[32:34], ui[12:14], up[24:28], up[28:32], ui[8:12]])
    v0 = collect(part, "x").astype(BF)

    v0, up, ui, upper_bwd = lax.optimization_barrier((v0, up, ui, upper_bwd))
    (p_ui3, p_u23, p_ui2, p_u1, p_ui1), = gather([upper_bwd], ((1, 1, 1, 2, 1),))
    leaf_bwd = spread_leaf([up[0:8], up[8:16], up[16:24], ui[0:8]])
    update = parity(collect(by_rows(p_l01, v0).astype(BF), "y0"))
    part = by_cols(p_li1, (parity(b1) - update).astype(BF)).astype(BF)
    v1 = collect(part, "x").astype(BF)
    v1, leaf_bwd = lax.optimization_barrier((v1, leaf_bwd))
    (p_u0, p_ui0), = gather([leaf_bwd], ((3, 1),))
    v1 = lax.optimization_barrier(collect(v1, "y0").astype(BF))

    leaf_part = by_rows(p_l0, v0).reshape(2, 4, 2, n, 64)
    node_part = by_rows(p_l1, v1).reshape(2, 4, 1, n, 64)
    part = (leaf_part + jnp.where(mine, node_part, 0.0)).astype(BF).reshape(2, 8, n, 64)
    quad = share(part, ("y1", "y0"), 4).astype(F32).reshape(4, 2, 8, n, 64).sum(0)
    v2 = sum_x(by_cols(p_li2, (b2 - quad[0]).astype(BF))).astype(BF)

    part = (parity(quad[1]) + by_rows(p_l23, v2)).astype(BF)
    update = share(part, ("y2", "y0"), 4).astype(F32).reshape(2, 2, 4, n, 64).sum(0)
    update = jnp.swapaxes(update, 0, 1).reshape(8, n, 64)
    v3 = sum_x(by_cols(p_li3, (b3 - update).astype(BF))).astype(BF)

    def collect_group(part):
        return collect(collect(part.astype(BF), "x").astype(BF), "y0")

    s3 = by_rows(p_ui3, v3).astype(BF)
    res = v2.astype(F32) - collect_group(by_cols(p_u23, s3))
    s2 = by_rows(p_ui2, res.astype(BF)).astype(BF)
    res = v1.astype(F32) - collect_group(by_cols(p_u1, jnp.concatenate([s2, s3], axis=0)))
    s1 = by_rows(p_ui1, res.astype(BF)).astype(BF)

    uppers = lax.all_gather(jnp.stack([s1, s2, s3]), "y0", axis=0, tiled=False)
    uppers = jnp.transpose(uppers, (1, 2, 0, 3, 4)).reshape(3, 8, n, 64)
    part = by_cols(p_u0, uppers.reshape(24, n, 64))
    res = (v0.astype(F32) - sum_x(part)).astype(BF)
    s0 = by_rows(p_ui0, res).astype(BF)

    got = swap(jnp.stack([s0, uppers[0], uppers[1]], axis=1), Y)
    last = lax.dynamic_index_in_dim(uppers[2], yi, 0, keepdims=True)
    out = jnp.concatenate([got[:, 0], got[0::2, 1], got[0::4, 2], last], axis=0)
    return jnp.swapaxes(out, 1, 2)


def solution(mesh):
    fine = Mesh(mesh.devices.reshape(8, 2, 4, 2, 2, 2), ("z", "core", "x", "y2", "y1", "y0"))
    spec = P(None, ("x", "y2", "y1", "y0"), ("z", "core"))
    return jax.shard_map(local, mesh=fine, in_specs=(spec,) * 7, out_specs=spec, check_vma=False)
```

time: 342 us -> 319 us (0.933)
  waiting for transfers between devices: 89.6 us -> 70.1 us
  blocking collectives: 119 us -> 137 us
  starting transfers between devices: 51.3 us -> 38.7 us
  local copies, waits for them, and re-layouts: 19.1 us -> 12.9 us
  matrix products: 40.9 us -> 35 us
    all_gather x0 -> x9, blocking collectives: none -> 85.7 us  [the longest x8 80 us: collect(): return lax.all_gather(part, axis, axis=0, tiled=False).astype(F32).sum(0)]
    all_to_all x11 -> x4, blocking collectives: 119 us -> 51.5 us  [swap(): return lax.all_to_all(blocks, axes, 0, 0, tiled=True)]
    all_to_all x12 -> x8, waiting for transfers between devices: 79.9 us -> 63.1 us  [swap(): return lax.all_to_all(blocks, axes, 0, 0, tiled=True)]
    all_to_all x12 -> x8, starting transfers between devices: 51.3 us -> 38.6 us  [swap(): return lax.all_to_all(blocks, axes, 0, 0, tiled=True)]
    unnamed x26 -> x23, local copies, waits for them, and re-layouts: 7.65 us -> 2.8 us
    dot_general x10 -> x7, matrix products: 19.1 us -> 15.5 us  [by_cols(): jnp.einsum('snr,psrc->pnc', vector, panel, preferred_element_type=F32)]
    all_gather x3 -> x4, waiting for transfers between devices: 9.61 us -> 6.99 us  [gather(): full = lax.all_gather(flat, PROW, axis=0, tiled=False)]
    dot_general x10 -> x8, matrix products: 21.8 us -> 19.5 us  [by_rows(): jnp.einsum('pnc,psrc->snr', vector, panel, preferred_element_type=F32)]
  transfers between devices with their start and end apart: 15 -> 12, of which waited for: 13 -> 7; matrix products, arithmetic and copies ran while one was open for 12% -> 13% of each run, Pallas kernels for 0% -> 0%
where the time goes in v2:
time: 319 us; the launch traced here: 317 us
  blocking collectives  137 us (43%)
  waiting for transfers between devices  70.1 us (22%)
  starting transfers between devices  38.7 us (12%)
  matrix products  35 us (11%)
  between operations  15.4 us (5%)
  local copies, waits for them, and re-layouts  12.9 us (4%)
  other arithmetic  7.87 us (2%)
    all_gather x8, blocking collectives, collect(): return lax.all_gather(part, axis, axis=0, tiled=False).astype(F32).sum(0)  80 us
    all_to_all x8, waiting for transfers between devices, swap(): return lax.all_to_all(blocks, axes, 0, 0, tiled=True)  63.1 us
    all_to_all x4, blocking collectives, swap(): return lax.all_to_all(blocks, axes, 0, 0, tiled=True)  51.5 us
    all_to_all x8, starting transfers between devices, swap(): return lax.all_to_all(blocks, axes, 0, 0, tiled=True)  38.6 us
    dot_general x8, matrix products, by_rows(): jnp.einsum('pnc,psrc->snr', vector, panel, preferred_element_type=F32)  19.5 us
    dot_general x7, matrix products, by_cols(): jnp.einsum('snr,psrc->pnc', vector, panel, preferred_element_type=F32)  15.5 us
    all_gather x4, waiting for transfers between devices, gather(): full = lax.all_gather(flat, PROW, axis=0, tiled=False)  6.99 us
  transfers between devices with their start and end apart: 12, of which 7 were waited for; matrix products, arithmetic and copies ran while one was open for 13% of the time, Pallas kernels for 0%

profile of v2, /device:TPU:2, one launch (start us, length us, event | category | flops | bytes accessed | tf_op | source)
XLA Modules:
  0.0 317.2 jit_solution(803129142301599016)
XLA Ops:
  10.0 7.2 %all-to-all-start = ((bf16[8,3,64,128]{3,2,1,0:T(8,128)(2,1)}), bf16[8,3,64,128]{3,2,1,0:T(8,128)(2,1)S(1)}, u32[]{:S(2)}, u32[]{:S(2)}) async-start(bf16[8,3,64,128]{3,2,1,0:T(8,128)(2,1)} %pad_maximum_fusion.3), calls=%async_computation | async-start | bytes 786432 | tf_op jit(solution)/shard_map/all_to_all | solution.py:14
  17.3 14.6 %all-to-all-done = bf16[8,3,64,128]{3,2,1,0:T(8,128)(2,1)S(1)} async-done(((bf16[8,3,64,128]{3,2,1,0:T(8,128)(2,1)}), bf16[8,3,64,128]{3,2,1,0:T(8,128)(2,1)S(1)}, u32[]{:S(2)}, u32[]{:S(2)}) %all-to-all-start) | async-done | bytes 393248 | tf_op jit(solution)/shard_map/all_to_all | solution.py:14
  40.0 8.0 %all-to-all-done.3 = bf16[4,3,64,128]{3,2,1,0:T(8,128)(2,1)S(1)} async-done(((bf16[4,3,64,128]{3,2,1,0:T(8,128)(2,1)}), bf16[4,3,64,128]{3,2,1,0:T(8,128)(2,1)S(1)}, u32[]{:S(2)}, u32[]{:S(2)}) %all-to-all-start.3) | async-done | bytes 196640 | tf_op jit(solution)/shard_map/all_to_all | solution.py:14
  51.5 15.7 %all-to-all-done.2 = bf16[8,4,64,128]{3,2,1,0:T(8,128)(2,1)S(1)} async-done(((bf16[8,4,64,128]{3,2,1,0:T(8,128)(2,1)}), bf16[8,4,64,128]{3,2,1,0:T(8,128)(2,1)S(1)}, u32[]{:S(2)}, u32[]{:S(2)}) %all-to-all-start.2) | async-done | bytes 524320 | tf_op jit(solution)/shard_map/all_to_all | solution.py:14
  68.7 11.8 %all_to_all.60 = bf16[8,2,5120]{2,1,0:T(2,128)(2,1)S(1)} all-to-all(bf16[8,2,5120]{2,1,0:T(2,128)(2,1)S(1)} %reshape.297), channel_id=1, replica_groups=mesh['z'=8,'core'=2,'x'=4,'y2'=2,'y1'=2,'y0'=2] {'y2','y1','y0'}, dimensions={0} | all-to-all | bytes 327680 | tf_op jit(solution)/shard_map/all_to_all | solution.py:14
  90.0 13.9 %all-gather.1 = bf16[64,40,128]{2,1,0:T(8,128)(2,1)S(1)} all-gather(bf16[16,40,128]{2,1,0:T(8,128)(2,1)S(1)} %fusion.13), channel_id=3, replica_groups=mesh['z'=8,'core'=2,'x'=4,'y2'=2,'y1'=2,'y0'=2] {'x'}, dimensions={0}, use_global_device_ids=true | all-gather | bytes 819200 | tf_op jit(solution)/shard_map/all_gather | solution.py:50
  105.8 7.2 %all-to-all-start.5 = ((bf16[8,4,64,128]{3,2,1,0:T(8,128)(2,1)}), bf16[8,4,64,128]{3,2,1,0:T(8,128)(2,1)S(1)}, u32[]{:S(2)}, u32[]{:S(2)}) async-start(bf16[8,4,64,128]{3,2,1,0:T(8,128)(2,1)} %copy.150), calls=%async_computation.5 | async-start | bytes 1048576 | tf_op jit(solution)/shard_map/all_to_all | solution.py:14
  115.7 9.0 %all-gather.2 = bf16[16,40,64]{2,1,0:T(8,128)(2,1)S(1)} all-gather(bf16[8,40,64]{2,1,0:T(8,128)(2,1)S(1)} %fusion.17), channel_id=4, replica_groups=mesh['z'=8,'core'=2,'x'=4,'y2'=2,'y1'=2,'y0'=2] {'y0'}, dimensions={0}, use_global_device_ids=true | all-gather | bytes 122880 | tf_op jit(solution)/shard_map/all_gather | solution.py:50
  126.4 13.0 %all-gather.3 = bf16[64,40,128]{2,1,0:T(8,128)(2,1)S(1)} all-gather(bf16[16,40,128]{2,1,0:T(8,128)(2,1)S(1)} %fusion.12), channel_id=5, replica_groups=mesh['z'=8,'core'=2,'x'=4,'y2'=2,'y1'=2,'y0'=2] {'x'}, dimensions={0}, use_global_device_ids=true | all-gather | bytes 819200 | tf_op jit(solution)/shard_map/all_gather | solution.py:50
  140.5 6.0 %all-gather.4 = bf16[32,40,128]{2,1,0:T(8,128)(2,1)S(1)} all-gather(bf16[16,40,128]{2,1,0:T(8,128)(2,1)S(1)} %reduce_sum.140), channel_id=6, replica_groups=mesh['z'=8,'core'=2,'x'=4,'y2'=2,'y1'=2,'y0'=2] {'y0'}, dimensions={0}, use_global_device_ids=true | all-gather | bytes 491520 | tf_op jit(solution)/shard_map/all_gather | solution.py:50
  146.6 6.9 %all-gather.22.cloned.1.call-done = bf16[704,64,128]{2,1,0:T(8,128)(2,1)} async-done(((bf16[44,64,128]{2,1,0:T(8,128)(2,1)}), bf16[704,64,128]{2,1,0:T(8,128)(2,1)}) %all-gather.22.cloned.1.call-update) | async-done | bytes 11534352 | tf_op jit(solution)/shard_map/all_gather | solution.py:38
  161.1 15.1 %all_to_all.61 = bf16[4,2,20480]{2,1,0:T(2,128)(2,1)S(1)} all-to-all(bf16[4,2,20480]{2,1,0:T(2,128)(2,1)S(1)} %reshape.299), channel_id=1, replica_groups=mesh['z'=8,'core'=2,'x'=4,'y2'=2,'y1'=2,'y0'=2] {'y1','y0'}, dimensions={0} | all-to-all | bytes 655360 | tf_op jit(solution)/shard_map/all_to_all | solution.py:14
  179.8 4.8 %all-to-all-start.7 = ((bf16[4,16,40,128]{3,2,1,0:T(8,128)(2,1)}), bf16[4,16,40,128]{3,2,1,0:T(8,128)(2,1)S(1)}, u32[]{:S(2)}, u32[]{:S(2)}) async-start(bf16[4,16,40,128]{3,2,1,0:T(8,128)(2,1)} %broadcast_in_dim.240), calls=%async_computation.7 | async-start | bytes 1310720 | tf_op jit(solution)/shard_map/all_to_all | solution.py:14
  184.6 8.6 %all-to-all-done.7 = bf16[4,16,40,128]{3,2,1,0:T(8,128)(2,1)S(1)} async-done(((bf16[4,16,40,128]{3,2,1,0:T(8,128)(2,1)}), bf16[4,16,40,128]{3,2,1,0:T(8,128)(2,1)S(1)}, u32[]{:S(2)}, u32[]{:S(2)}) %all-to-all-start.7) | async-done | bytes 655392 | tf_op jit(solution)/shard_map/all_to_all | solution.py:14
  195.3 13.4 %all_to_all.62 = bf16[4,2,5120]{2,1,0:T(2,128)(2,1)S(1)} all-to-all(bf16[4,2,5120]{2,1,0:T(2,128)(2,1)S(1)} %reshape.301), channel_id=1, replica_groups=mesh['z'=8,'core'=2,'x'=4,'y2'=2,'y1'=2,'y0'=2] {'y2','y0'}, dimensions={0} | all-to-all | bytes 163840 | tf_op jit(solution)/shard_map/all_to_all | solution.py:14
  211.2 11.2 %all_to_all.63 = bf16[4,16,40,128]{3,2,1,0:T(8,128)(2,1)S(1)} all-to-all(bf16[4,16,40,128]{3,2,1,0:T(8,128)(2,1)S(1)} %broadcast_in_dim.242), channel_id=1, replica_groups=mesh['z'=8,'core'=2,'x'=4,'y2'=2,'y1'=2,'y0'=2] {'x'}, dimensions={0} | all-to-all | bytes 1310720 | tf_op jit(solution)/shard_map/all_to_all | solution.py:14
  225.9 13.0 %all-gather.6 = bf16[64,40,128]{2,1,0:T(8,128)(2,1)S(1)} all-gather(bf16[16,40,128]{2,1,0:T(8,128)(2,1)S(1)} %fusion.9), channel_id=8, replica_groups=mesh['z'=8,'core'=2,'x'=4,'y2'=2,'y1'=2,'y0'=2] {'x'}, dimensions={0}, use_global_device_ids=true | all-gather | bytes 819200 | tf_op jit(solution)/shard_map/all_gather | solution.py:50
  239.0 6.0 %all-gather.7 = bf16[32,40,128]{2,1,0:T(8,128)(2,1)S(1)} all-gather(bf16[16,40,128]{2,1,0:T(8,128)(2,1)S(1)} %reduce_sum.146), channel_id=9, replica_groups=mesh['z'=8,'core'=2,'x'=4,'y2'=2,'y1'=2,'y0'=2] {'y0'}, dimensions={0}, use_global_device_ids=true | all-gather | bytes 491520 | tf_op jit(solution)/shard_map/all_gather | solution.py:50
  249.0 13.1 %all-gather.8 = bf16[64,40,128]{2,1,0:T(8,128)(2,1)S(1)} all-gather(bf16[16,40,128]{2,1,0:T(8,128)(2,1)S(1)} %fusion.8), channel_id=10, replica_groups=mesh['z'=8,'core'=2,'x'=4,'y2'=2,'y1'=2,'y0'=2] {'x'}, dimensions={0}, use_global_device_ids=true | all-gather | bytes 819200 | tf_op jit(solution)/shard_map/all_gather | solution.py:50
  262.2 6.0 %all-gather.9 = bf16[32,40,128]{2,1,0:T(8,128)(2,1)S(1)} all-gather(bf16[16,40,128]{2,1,0:T(8,128)(2,1)S(1)} %reduce_sum.148), channel_id=11, replica_groups=mesh['z'=8,'core'=2,'x'=4,'y2'=2,'y1'=2,'y0'=2] {'y0'}, dimensions={0}, use_global_device_ids=true | all-gather | bytes 491520 | tf_op jit(solution)/shard_map/all_gather | solution.py:50
  270.1 5.7 %all-gather.10 = bf16[6,4,40,64]{3,2,1,0:T(8,128)(2,1)S(1)} all-gather(bf16[3,4,40,64]{3,2,1,0:T(8,128)(2,1)S(1)} %pad_maximum_fusion.8), channel_id=12, replica_groups=mesh['z'=8,'core'=2,'x'=4,'y2'=2,'y1'=2,'y0'=2] {'y0'}, dimensions={0}, use_global_device_ids=true | all-gather | bytes 184320 | tf_op jit(solution)/shard_map/all_gather | solution.py:136
  280.8 5.6 %all-to-all-start.10 = ((bf16[4,16,40,128]{3,2,1,0:T(8,128)(2,1)}), bf16[4,16,40,128]{3,2,1,0:T(8,128)(2,1)S(1)}, u32[]{:S(2)}, u32[]{:S(2)}) async-start(bf16[4,16,40,128]{3,2,1,0:T(8,128)(2,1)} %broadcast_in_dim.243), calls=%async_computation.10 | async-start | bytes 1310720 | tf_op jit(solution)/shard_map/all_to_all | solution.py:14
  286.5 7.3 %all-to-all-done.10 = bf16[4,16,40,128]{3,2,1,0:T(8,128)(2,1)S(1)} async-done(((bf16[4,16,40,128]{3,2,1,0:T(8,128)(2,1)}), bf16[4,16,40,128]{3,2,1,0:T(8,128)(2,1)S(1)}, u32[]{:S(2)}, u32[]{:S(2)}) %all-to-all-start.10) | async-done | bytes 655392 | tf_op jit(solution)/shard_map/all_to_all | solution.py:14
  300.9 8.9 %all-to-all-done.11 = bf16[8,2,3840]{2,1,0:T(2,128)(2,1)S(1)} async-done(((bf16[8,2,3840]{2,1,0:T(2,128)(2,1)}), bf16[8,2,3840]{2,1,0:T(2,128)(2,1)S(1)}, u32[]{:S(2)}, u32[]{:S(2)}) %all-to-all-start.11) | async-done | bytes 122912 | tf_op jit(solution)/shard_map/all_to_all | solution.py:14
  (153 shorter events, 69.8 us)
Async XLA Ops:
  6.5 32.4 %copy-start.2 = (bf16[15,64,128]{2,1,0:T(8,128)(2,1)S(1)}, bf16[15,64,128]{2,1,0:T(8,128)(2,1)}, u32[]{:S(2)}) copy-start(bf16[15,64,128]{2,1,0:T(8,128)(2,1)} %param.12) | copy-start | bytes 737284
  6.5 32.5 %slice-start.1 = ((bf16[15,64,128]{2,1,0:T(8,128)(2,1)}), bf16[2,64,128]{2,1,0:T(8,128)(2,1)S(1)}, s32[]{:S(2)}) async-start(bf16[15,64,128]{2,1,0:T(8,128)(2,1)} %param.12), calls=%async_computation.17 | async-start | bytes 65536 | tf_op jit(solution)/shard_map/slice | solution.py:92
  10.0 58.2 %copy-start.3 = (bf16[15,64,40]{1,2,0:T(8,128)(2,1)S(1)}, bf16[15,64,40]{1,2,0:T(8,128)(2,1)}, u32[]{:S(2)}) copy-start(bf16[15,64,40]{1,2,0:T(8,128)(2,1)} %param.7) | copy-start | bytes 230404
  10.0 21.9 %all-to-all-start = ((bf16[8,3,64,128]{3,2,1,0:T(8,128)(2,1)}), bf16[8,3,64,128]{3,2,1,0:T(8,128)(2,1)S(1)}, u32[]{:S(2)}, u32[]{:S(2)}) async-start(bf16[8,3,64,128]{3,2,1,0:T(8,128)(2,1)} %pad_maximum_fusion.3), calls=%async_computation | async-start | bytes 786432 | tf_op jit(solution)/shard_map/all_to_all | solution.py:14
  17.3 65.9 %all-gather.20.cloned.1.call-start = ((), (), s32[]{:S(2)}) async-start(), calls=%async_computation.14 | async-start | bytes 5570560 | tf_op jit(solution)/shard_map/all_gather | solution.py:38
  35.6 12.3 %all-to-all-start.3 = ((bf16[4,3,64,128]{3,2,1,0:T(8,128)(2,1)}), bf16[4,3,64,128]{3,2,1,0:T(8,128)(2,1)S(1)}, u32[]{:S(2)}, u32[]{:S(2)}) async-start(bf16[4,3,64,128]{3,2,1,0:T(8,128)(2,1)} %copy.145), calls=%async_computation.3 | async-start | bytes 393216 | tf_op jit(solution)/shard_map/all_to_all | solution.py:14
  39.1 46.3 %copy-start.4 = (s32[34,1,2]{0,2,1:T(2,128)S(1)}, s32[34,1,2]{0,2,1:T(2,128)}, u32[]{:S(2)}) copy-start(s32[34,1,2]{0,2,1:T(2,128)} %param.11) | copy-start | bytes 820
  39.1 46.4 %copy-start = (bf16[34,64,128]{2,1,0:T(8,128)(2,1)S(1)}, bf16[34,64,128]{2,1,0:T(8,128)(2,1)}, u32[]{:S(2)}) copy-start(bf16[34,64,128]{2,1,0:T(8,128)(2,1)} %param.10) | copy-start | bytes 1671172
  39.9 45.6 %copy-start.1 = (bf16[15,64,128]{2,1,0:T(8,128)(2,1)S(1)}, bf16[15,64,128]{2,1,0:T(8,128)(2,1)}, u32[]{:S(2)}) copy-start(bf16[15,64,128]{2,1,0:T(8,128)(2,1)} %param.13) | copy-start | bytes 737284
  47.9 19.3 %all-to-all-start.2 = ((bf16[8,4,64,128]{3,2,1,0:T(8,128)(2,1)}), bf16[8,4,64,128]{3,2,1,0:T(8,128)(2,1)S(1)}, u32[]{:S(2)}, u32[]{:S(2)}) async-start(bf16[8,4,64,128]{3,2,1,0:T(8,128)(2,1)} %pad_maximum_fusion.1), calls=%async_computation.2 | async-start | bytes 1048576 | tf_op jit(solution)/shard_map/all_to_all | solution.py:14
  51.4 34.2 %slice-start = ((bf16[15,64,128]{2,1,0:T(8,128)(2,1)}), bf16[2,64,128]{2,1,0:T(8,128)(2,1)S(1)}, s32[]{:S(2)}) async-start(bf16[15,64,128]{2,1,0:T(8,128)(2,1)} %param.13), calls=%async_computation.16 | async-start | bytes 65536 | tf_op jit(solution)/shard_map/slice | solution.py:103
  51.4 102.1 %all-gather.22.cloned.1.call-start = ((), (), s32[]{:S(2)}) async-start(), calls=%async_computation.15 | async-start | bytes 12255232 | tf_op jit(solution)/shard_map/all_gather | solution.py:38
  86.5 17.5 %all-to-all-start.4 = ((bf16[4,6,64,128]{3,2,1,0:T(8,128)(2,1)}), bf16[4,6,64,128]{3,2,1,0:T(8,128)(2,1)S(1)}, u32[]{:S(2)}, u32[]{:S(2)}) async-start(bf16[4,6,64,128]{3,2,1,0:T(8,128)(2,1)} %copy.147), calls=%async_computation.4 | async-start | bytes 786432 | tf_op jit(solution)/shard_map/all_to_all | solution.py:14
  90.0 132.5 %all-gather.18.cloned.1.call-start = ((), (), s32[]{:S(2)}) async-start(), calls=%async_computation.13 | async-start | bytes 6684672 | tf_op jit(solution)/shard_map/all_gather | solution.py:38
  105.8 33.7 %all-to-all-start.5 = ((bf16[8,4,64,128]{3,2,1,0:T(8,128)(2,1)}), bf16[8,4,64,128]{3,2,1,0:T(8,128)(2,1)S(1)}, u32[]{:S(2)}, u32[]{:S(2)}) async-start(bf16[8,4,64,128]{3,2,1,0:T(8,128)(2,1)} %copy.150), calls=%async_computation.5 | async-start | bytes 1048576 | tf_op jit(solution)/shard_map/all_to_all | solution.py:14
  113.0 162.9 %all-gather.16.cloned.1.call-start = ((), (), s32[]{:S(2)}) async-start(), calls=%async_computation.12 | async-start | bytes 8912896 | tf_op jit(solution)/shard_map/all_gather | solution.py:38
  179.8 13.4 %all-to-all-start.7 = ((bf16[4,16,40,128]{3,2,1,0:T(8,128)(2,1)}), bf16[4,16,40,128]{3,2,1,0:T(8,128)(2,1)S(1)}, u32[]{:S(2)}, u32[]{:S(2)}) async-start(bf16[4,16,40,128]{3,2,1,0:T(8,128)(2,1)} %broadcast_in_dim.240), calls=%async_computation.7 | async-start | bytes 1310720 | tf_op jit(solution)/shard_map/all_to_all | solution.py:14
  280.8 12.9 %all-to-all-start.10 = ((bf16[4,16,40,128]{3,2,1,0:T(8,128)(2,1)}), bf16[4,16,40,128]{3,2,1,0:T(8,128)(2,1)S(1)}, u32[]{:S(2)}, u32[]{:S(2)}) async-start(bf16[4,16,40,128]{3,2,1,0:T(8,128)(2,1)} %broadcast_in_dim.243), calls=%async_computation.10 | async-start | bytes 1310720 | tf_op jit(solution)/shard_map/all_to_all | solution.py:14
  297.4 12.3 %all-to-all-start.11 = ((bf16[8,2,3840]{2,1,0:T(2,128)(2,1)}), bf16[8,2,3840]{2,1,0:T(2,128)(2,1)S(1)}, u32[]{:S(2)}, u32[]{:S(2)}) async-start(bf16[8,2,3840]{2,1,0:T(2,128)(2,1)} %reshape.303), calls=%async_computation.11 | async-start | bytes 245760 | tf_op jit(solution)/shard_map/all_to_all | solution.py:14
Sparse Core Ops, SparseCore 0:
  33.0 46.1 all-gather.19
  81.3 72.1 all-gather.21
  155.6 47.4 all-gather.17
  205.1 57.3 all-gather.15

commit v3 on v2

--- a/solution.py
+++ b/solution.py
@@ -89,9 +89,10 @@
     n = b0.shape[1]
     b1, b2, b3 = (nodes[:, k].astype(F32) for k in (1, 2, 3))
 
-    leaf_fwd = spread_leaf([low[8:16], low[16:24], jnp.repeat(li[12:14], 4, 0), jnp.repeat(li[14:15], 8, 0)])
+    leaf_fwd = spread_leaf([low[8:16], low[16:24], jnp.repeat(li[12:14], 4, 0), jnp.repeat(li[14:15], 8, 0),
+                            jnp.repeat(ui[8:12], 2, 0)])
     upper_fwd = spread_upper([low[24:28], low[28:32], low[32:34]])
-    p_leaf, p_upper = gather([leaf_fwd, upper_fwd], ((2, 1, 1), (2, 1)))
+    p_leaf, p_upper = gather([leaf_fwd[0:4], upper_fwd], ((2, 1, 1), (2, 1)))
     (p_l0, p_li2, p_li3), (p_l1, p_l23) = p_leaf, p_upper
 
     mine = lax.broadcasted_iota(jnp.int32, (1, 1, 2, 1, 1), 2) == y0
@@ -100,11 +101,11 @@
     part = by_cols(p_li0, b0 + nothing).astype(BF)
     part, upper_panels, upper_pattern, ui = lax.optimization_barrier((part, upper_panels, upper_pattern, ui))
     up = masked(upper_panels, upper_pattern)
-    upper_bwd = spread_upper([ui[14:15], up[32:34], ui[12:14], up[24:28], up[28:32], ui[8:12]])
+    upper_bwd = spread_upper([ui[14:15], up[32:34], ui[12:14], up[24:28], up[28:32]])
     v0 = collect(part, "x").astype(BF)
 
     v0, up, ui, upper_bwd = lax.optimization_barrier((v0, up, ui, upper_bwd))
-    (p_ui3, p_u23, p_ui2, p_u1, p_ui1), = gather([upper_bwd], ((1, 1, 1, 2, 1),))
+    (p_ui1,), (p_ui3, p_u23, p_ui2, p_u1) = gather([leaf_fwd[4:5], upper_bwd], ((1,), (1, 1, 1, 2)))
     leaf_bwd = spread_leaf([up[0:8], up[8:16], up[16:24], ui[0:8]])
     update = parity(collect(by_rows(p_l01, v0).astype(BF), "y0"))
     part = by_cols(p_li1, (parity(b1) - update).astype(BF)).astype(BF)
@@ -130,11 +131,15 @@
     s3 = by_rows(p_ui3, v3).astype(BF)
     res = v2.astype(F32) - collect_group(by_cols(p_u23, s3))
     s2 = by_rows(p_ui2, res.astype(BF)).astype(BF)
-    res = v1.astype(F32) - collect_group(by_cols(p_u1, jnp.concatenate([s2, s3], axis=0)))
+    part = by_cols(p_u1, jnp.concatenate([s2, s3], axis=0)).astype(BF)
+    part = share(part, "x", 4).astype(F32).reshape(4, 16, n, 128).sum(0).astype(BF)
+    above = lax.all_gather(jnp.stack([s2, s3]), "y0", axis=0, tiled=False)
+    above = jnp.transpose(above, (1, 2, 0, 3, 4)).reshape(2, 8, n, 64)
+    part, above = lax.optimization_barrier((part, above))
+    res = v1.astype(F32) - collect(part, "y0")
     s1 = by_rows(p_ui1, res.astype(BF)).astype(BF)
 
-    uppers = lax.all_gather(jnp.stack([s1, s2, s3]), "y0", axis=0, tiled=False)
-    uppers = jnp.transpose(uppers, (1, 2, 0, 3, 4)).reshape(3, 8, n, 64)
+    uppers = jnp.concatenate([s1[None], above], axis=0)
     part = by_cols(p_u0, uppers.reshape(24, n, 64))
     res = (v0.astype(F32) - sum_x(part)).astype(BF)
     s0 = by_rows(p_ui0, res).astype(BF)

time: 319 us -> 316 us (level)
  blocking collectives: 137 us -> 123 us
  starting transfers between devices: 38.7 us -> 44.7 us
  local copies, waits for them, and re-layouts: 12.9 us -> 16.3 us
    all_gather x8 -> x7, blocking collectives: 80 us -> 65.4 us  [collect(): return lax.all_gather(part, axis, axis=0, tiled=False).astype(F32).sum(0)]
    all_to_all x8 -> x9, starting transfers between devices: 38.6 us -> 44.6 us  [swap(): return lax.all_to_all(blocks, axes, 0, 0, tiled=True)]
    all_to_all x8 -> x9, waiting for transfers between devices: 63.1 us -> 65.3 us  [swap(): return lax.all_to_all(blocks, axes, 0, 0, tiled=True)]
  transfers between devices with their start and end apart: 12 -> 13, of which waited for: 7 -> 8; matrix products, arithmetic and copies ran while one was open for 13% -> 15% of each run, Pallas kernels for 0% -> 0%
where the time goes in v3:
time: 316 us; the launch traced here: 314 us
  blocking collectives  123 us (39%)
  waiting for transfers between devices  71.1 us (22%)
  starting transfers between devices  44.7 us (14%)
  matrix products  36 us (11%)
  local copies, waits for them, and re-layouts  16.3 us (5%)
  between operations  15.2 us (5%)
  other arithmetic  7.82 us (2%)
    all_gather x7, blocking collectives, collect(): return lax.all_gather(part, axis, axis=0, tiled=False).astype(F32).sum(0)  65.4 us
    all_to_all x9, waiting for transfers between devices, swap(): return lax.all_to_all(blocks, axes, 0, 0, tiled=True)  65.3 us
    all_to_all x4, blocking collectives, swap(): return lax.all_to_all(blocks, axes, 0, 0, tiled=True)  51.4 us
    all_to_all x9, starting transfers between devices, swap(): return lax.all_to_all(blocks, axes, 0, 0, tiled=True)  44.6 us
    dot_general x8, matrix products, by_rows(): jnp.einsum('pnc,psrc->snr', vector, panel, preferred_element_type=F32)  20.5 us
    dot_general x7, matrix products, by_cols(): jnp.einsum('snr,psrc->pnc', vector, panel, preferred_element_type=F32)  15.5 us
  transfers between devices with their start and end apart: 13, of which 8 were waited for; matrix products, arithmetic and copies ran while one was open for 15% of the time, Pallas kernels for 0%

profile of v3, /device:TPU:2, one launch (start us, length us, event | category | flops | bytes accessed | tf_op | source)
XLA Modules:
  0.0 313.9 jit_solution(5902510068131741764)
XLA Ops:
  10.0 7.2 %all-to-all-start = ((bf16[8,3,64,128]{3,2,1,0:T(8,128)(2,1)}), bf16[8,3,64,128]{3,2,1,0:T(8,128)(2,1)S(1)}, u32[]{:S(2)}, u32[]{:S(2)}) async-start(bf16[8,3,64,128]{3,2,1,0:T(8,128)(2,1)} %pad_maximum_fusion.3), calls=%async_computation | async-start | bytes 786432 | tf_op jit(solution)/shard_map/all_to_all | solution.py:14
  17.3 14.6 %all-to-all-done = bf16[8,3,64,128]{3,2,1,0:T(8,128)(2,1)S(1)} async-done(((bf16[8,3,64,128]{3,2,1,0:T(8,128)(2,1)}), bf16[8,3,64,128]{3,2,1,0:T(8,128)(2,1)S(1)}, u32[]{:S(2)}, u32[]{:S(2)}) %all-to-all-start) | async-done | bytes 393248 | tf_op jit(solution)/shard_map/all_to_all | solution.py:14
  42.4 5.5 %all-to-all-done.3 = bf16[4,3,64,128]{3,2,1,0:T(8,128)(2,1)S(1)} async-done(((bf16[4,3,64,128]{3,2,1,0:T(8,128)(2,1)}), bf16[4,3,64,128]{3,2,1,0:T(8,128)(2,1)S(1)}, u32[]{:S(2)}, u32[]{:S(2)}) %all-to-all-start.3) | async-done | bytes 196640 | tf_op jit(solution)/shard_map/all_to_all | solution.py:14
  51.5 18.6 %all-to-all-done.2 = bf16[8,5,64,128]{3,2,1,0:T(8,128)(2,1)S(1)} async-done(((bf16[8,5,64,128]{3,2,1,0:T(8,128)(2,1)}), bf16[8,5,64,128]{3,2,1,0:T(8,128)(2,1)S(1)}, u32[]{:S(2)}, u32[]{:S(2)}) %all-to-all-start.2) | async-done | bytes 655392 | tf_op jit(solution)/shard_map/all_to_all | solution.py:14
  71.6 11.8 %all_to_all.65 = bf16[8,2,5120]{2,1,0:T(2,128)(2,1)S(1)} all-to-all(bf16[8,2,5120]{2,1,0:T(2,128)(2,1)S(1)} %reshape.308), channel_id=1, replica_groups=mesh['z'=8,'core'=2,'x'=4,'y2'=2,'y1'=2,'y0'=2] {'y2','y1','y0'}, dimensions={0} | all-to-all | bytes 327680 | tf_op jit(solution)/shard_map/all_to_all | solution.py:14
  92.8 13.4 %all-gather.1 = bf16[64,40,128]{2,1,0:T(8,128)(2,1)S(1)} all-gather(bf16[16,40,128]{2,1,0:T(8,128)(2,1)S(1)} %fusion.13), channel_id=3, replica_groups=mesh['z'=8,'core'=2,'x'=4,'y2'=2,'y1'=2,'y0'=2] {'x'}, dimensions={0}, use_global_device_ids=true | all-gather | bytes 819200 | tf_op jit(solution)/shard_map/all_gather | solution.py:50
  108.2 7.5 %all-to-all-start.5 = ((bf16[8,4,64,128]{3,2,1,0:T(8,128)(2,1)}), bf16[8,4,64,128]{3,2,1,0:T(8,128)(2,1)S(1)}, u32[]{:S(2)}, u32[]{:S(2)}) async-start(bf16[8,4,64,128]{3,2,1,0:T(8,128)(2,1)} %copy.154), calls=%async_computation.5 | async-start | bytes 1048576 | tf_op jit(solution)/shard_map/all_to_all | solution.py:14
  118.4 7.5 %all-gather.2 = bf16[16,40,64]{2,1,0:T(8,128)(2,1)S(1)} all-gather(bf16[8,40,64]{2,1,0:T(8,128)(2,1)S(1)} %fusion.18), channel_id=4, replica_groups=mesh['z'=8,'core'=2,'x'=4,'y2'=2,'y1'=2,'y0'=2] {'y0'}, dimensions={0}, use_global_device_ids=true | all-gather | bytes 122880 | tf_op jit(solution)/shard_map/all_gather | solution.py:50
  127.5 13.0 %all-gather.3 = bf16[64,40,128]{2,1,0:T(8,128)(2,1)S(1)} all-gather(bf16[16,40,128]{2,1,0:T(8,128)(2,1)S(1)} %fusion.12), channel_id=5, replica_groups=mesh['z'=8,'core'=2,'x'=4,'y2'=2,'y1'=2,'y0'=2] {'x'}, dimensions={0}, use_global_device_ids=true | all-gather | bytes 819200 | tf_op jit(solution)/shard_map/all_gather | solution.py:50
  141.6 6.0 %all-gather.5 = bf16[32,40,128]{2,1,0:T(8,128)(2,1)S(1)} all-gather(bf16[16,40,128]{2,1,0:T(8,128)(2,1)S(1)} %reduce_sum.140), channel_id=7, replica_groups=mesh['z'=8,'core'=2,'x'=4,'y2'=2,'y1'=2,'y0'=2] {'y0'}, dimensions={0}, use_global_device_ids=true | all-gather | bytes 491520 | tf_op jit(solution)/shard_map/all_gather | solution.py:50
  147.7 5.8 %all-gather.22.cloned.1.call-done = bf16[704,64,128]{2,1,0:T(8,128)(2,1)} async-done(((bf16[44,64,128]{2,1,0:T(8,128)(2,1)}), bf16[704,64,128]{2,1,0:T(8,128)(2,1)}) %all-gather.22.cloned.1.call-update) | async-done | bytes 11534352 | tf_op jit(solution)/shard_map/all_gather | solution.py:38
  161.0 15.1 %all_to_all.66 = bf16[4,2,20480]{2,1,0:T(2,128)(2,1)S(1)} all-to-all(bf16[4,2,20480]{2,1,0:T(2,128)(2,1)S(1)} %reshape.310), channel_id=1, replica_groups=mesh['z'=8,'core'=2,'x'=4,'y2'=2,'y1'=2,'y0'=2] {'y1','y0'}, dimensions={0} | all-to-all | bytes 655360 | tf_op jit(solution)/shard_map/all_to_all | solution.py:14
  179.7 4.8 %all-to-all-start.7 = ((bf16[4,16,40,128]{3,2,1,0:T(8,128)(2,1)}), bf16[4,16,40,128]{3,2,1,0:T(8,128)(2,1)S(1)}, u32[]{:S(2)}, u32[]{:S(2)}) async-start(bf16[4,16,40,128]{3,2,1,0:T(8,128)(2,1)} %broadcast_in_dim.249), calls=%async_computation.7 | async-start | bytes 1310720 | tf_op jit(solution)/shard_map/all_to_all | solution.py:14
  184.5 8.7 %all-to-all-done.7 = bf16[4,16,40,128]{3,2,1,0:T(8,128)(2,1)S(1)} async-done(((bf16[4,16,40,128]{3,2,1,0:T(8,128)(2,1)}), bf16[4,16,40,128]{3,2,1,0:T(8,128)(2,1)S(1)}, u32[]{:S(2)}, u32[]{:S(2)}) %all-to-all-start.7) | async-done | bytes 655392 | tf_op jit(solution)/shard_map/all_to_all | solution.py:14
  195.4 13.4 %all_to_all.67 = bf16[4,2,5120]{2,1,0:T(2,128)(2,1)S(1)} all-to-all(bf16[4,2,5120]{2,1,0:T(2,128)(2,1)S(1)} %reshape.312), channel_id=1, replica_groups=mesh['z'=8,'core'=2,'x'=4,'y2'=2,'y1'=2,'y0'=2] {'y2','y0'}, dimensions={0} | all-to-all | bytes 163840 | tf_op jit(solution)/shard_map/all_to_all | solution.py:14
  211.2 11.1 %all_to_all.68 = bf16[4,16,40,128]{3,2,1,0:T(8,128)(2,1)S(1)} all-to-all(bf16[4,16,40,128]{3,2,1,0:T(8,128)(2,1)S(1)} %broadcast_in_dim.251), channel_id=1, replica_groups=mesh['z'=8,'core'=2,'x'=4,'y2'=2,'y1'=2,'y0'=2] {'x'}, dimensions={0} | all-to-all | bytes 1310720 | tf_op jit(solution)/shard_map/all_to_all | solution.py:14
  225.9 13.4 %all-gather.7 = bf16[64,40,128]{2,1,0:T(8,128)(2,1)S(1)} all-gather(bf16[16,40,128]{2,1,0:T(8,128)(2,1)S(1)} %fusion.9), channel_id=9, replica_groups=mesh['z'=8,'core'=2,'x'=4,'y2'=2,'y1'=2,'y0'=2] {'x'}, dimensions={0}, use_global_device_ids=true | all-gather | bytes 819200 | tf_op jit(solution)/shard_map/all_gather | solution.py:50
  239.3 6.0 %all-gather.8 = bf16[32,40,128]{2,1,0:T(8,128)(2,1)S(1)} all-gather(bf16[16,40,128]{2,1,0:T(8,128)(2,1)S(1)} %reduce_sum.146), channel_id=10, replica_groups=mesh['z'=8,'core'=2,'x'=4,'y2'=2,'y1'=2,'y0'=2] {'y0'}, dimensions={0}, use_global_device_ids=true | all-gather | bytes 491520 | tf_op jit(solution)/shard_map/all_gather | solution.py:50
  250.3 5.2 %all-to-all-start.10 = ((bf16[4,16,40,128]{3,2,1,0:T(8,128)(2,1)}), bf16[4,16,40,128]{3,2,1,0:T(8,128)(2,1)S(1)}, u32[]{:S(2)}, u32[]{:S(2)}) async-start(bf16[4,16,40,128]{3,2,1,0:T(8,128)(2,1)} %broadcast_in_dim.252), calls=%async_computation.10 | async-start | bytes 1310720 | tf_op jit(solution)/shard_map/all_to_all | solution.py:14
  255.5 5.8 %all-gather.9 = bf16[4,4,40,64]{3,2,1,0:T(8,128)(2,1)S(1)} all-gather(bf16[2,4,40,64]{3,2,1,0:T(8,128)(2,1)S(1)} %pad_maximum_fusion.9), channel_id=11, replica_groups=mesh['z'=8,'core'=2,'x'=4,'y2'=2,'y1'=2,'y0'=2] {'y0'}, dimensions={0}, use_global_device_ids=true | all-gather | bytes 122880 | tf_op jit(solution)/shard_map/all_gather | solution.py:136
  262.9 6.2 %all-gather.10 = bf16[32,40,128]{2,1,0:T(8,128)(2,1)S(1)} all-gather(bf16[16,40,128]{2,1,0:T(8,128)(2,1)S(1)} %reduce_sum.148), channel_id=12, replica_groups=mesh['z'=8,'core'=2,'x'=4,'y2'=2,'y1'=2,'y0'=2] {'y0'}, dimensions={0}, use_global_device_ids=true | all-gather | bytes 491520 | tf_op jit(solution)/shard_map/all_gather | solution.py:50
  276.8 4.9 %all-to-all-start.11 = ((bf16[4,16,40,128]{3,2,1,0:T(8,128)(2,1)}), bf16[4,16,40,128]{3,2,1,0:T(8,128)(2,1)S(1)}, u32[]{:S(2)}, u32[]{:S(2)}) async-start(bf16[4,16,40,128]{3,2,1,0:T(8,128)(2,1)} %broadcast_in_dim.254), calls=%async_computation.11 | async-start | bytes 1310720 | tf_op jit(solution)/shard_map/all_to_all | solution.py:14
  281.8 7.3 %all-to-all-done.11 = bf16[4,16,40,128]{3,2,1,0:T(8,128)(2,1)S(1)} async-done(((bf16[4,16,40,128]{3,2,1,0:T(8,128)(2,1)}), bf16[4,16,40,128]{3,2,1,0:T(8,128)(2,1)S(1)}, u32[]{:S(2)}, u32[]{:S(2)}) %all-to-all-start.11) | async-done | bytes 655392 | tf_op jit(solution)/shard_map/all_to_all | solution.py:14
  297.4 9.0 %all-to-all-done.12 = bf16[8,2,3840]{2,1,0:T(2,128)(2,1)S(1)} async-done(((bf16[8,2,3840]{2,1,0:T(2,128)(2,1)}), bf16[8,2,3840]{2,1,0:T(2,128)(2,1)S(1)}, u32[]{:S(2)}, u32[]{:S(2)}) %all-to-all-start.12) | async-done | bytes 122912 | tf_op jit(solution)/shard_map/all_to_all | solution.py:14
  (160 shorter events, 77.0 us)
Async XLA Ops:
  6.5 33.8 %slice-start.2 = ((bf16[15,64,128]{2,1,0:T(8,128)(2,1)}), bf16[2,64,128]{2,1,0:T(8,128)(2,1)S(1)}, s32[]{:S(2)}) async-start(bf16[15,64,128]{2,1,0:T(8,128)(2,1)} %param.12), calls=%async_computation.19 | async-start | bytes 65536 | tf_op jit(solution)/shard_map/slice | solution.py:92
  6.5 34.5 %copy-start.2 = (bf16[15,64,128]{2,1,0:T(8,128)(2,1)S(1)}, bf16[15,64,128]{2,1,0:T(8,128)(2,1)}, u32[]{:S(2)}) copy-start(bf16[15,64,128]{2,1,0:T(8,128)(2,1)} %param.12) | copy-start | bytes 737284
  6.5 35.1 %slice-start = ((bf16[15,64,128]{2,1,0:T(8,128)(2,1)}), bf16[4,64,128]{2,1,0:T(8,128)(2,1)S(1)}, s32[]{:S(2)}) async-start(bf16[15,64,128]{2,1,0:T(8,128)(2,1)} %param.13), calls=%async_computation.17 | async-start | bytes 131072 | tf_op jit(solution)/shard_map/slice | solution.py:93
  10.0 61.1 %copy-start.3 = (bf16[15,64,40]{1,2,0:T(8,128)(2,1)S(1)}, bf16[15,64,40]{1,2,0:T(8,128)(2,1)}, u32[]{:S(2)}) copy-start(bf16[15,64,40]{1,2,0:T(8,128)(2,1)} %param.7) | copy-start | bytes 230404
  10.0 21.9 %all-to-all-start = ((bf16[8,3,64,128]{3,2,1,0:T(8,128)(2,1)}), bf16[8,3,64,128]{3,2,1,0:T(8,128)(2,1)S(1)}, u32[]{:S(2)}, u32[]{:S(2)}) async-start(bf16[8,3,64,128]{3,2,1,0:T(8,128)(2,1)} %pad_maximum_fusion.3), calls=%async_computation | async-start | bytes 786432 | tf_op jit(solution)/shard_map/all_to_all | solution.py:14
  17.3 68.8 %all-gather.18.cloned.1.call-start = ((), (), s32[]{:S(2)}) async-start(), calls=%async_computation.14 | async-start | bytes 5570560 | tf_op jit(solution)/shard_map/all_gather | solution.py:38
  35.6 12.3 %all-to-all-start.3 = ((bf16[4,3,64,128]{3,2,1,0:T(8,128)(2,1)}), bf16[4,3,64,128]{3,2,1,0:T(8,128)(2,1)S(1)}, u32[]{:S(2)}, u32[]{:S(2)}) async-start(bf16[4,3,64,128]{3,2,1,0:T(8,128)(2,1)} %copy.148), calls=%async_computation.3 | async-start | bytes 393216 | tf_op jit(solution)/shard_map/all_to_all | solution.py:14
  39.6 48.5 %copy-start.4 = (s32[34,1,2]{0,2,1:T(2,128)S(1)}, s32[34,1,2]{0,2,1:T(2,128)}, u32[]{:S(2)}) copy-start(s32[34,1,2]{0,2,1:T(2,128)} %param.11) | copy-start | bytes 820
  39.6 48.6 %copy-start = (bf16[34,64,128]{2,1,0:T(8,128)(2,1)S(1)}, bf16[34,64,128]{2,1,0:T(8,128)(2,1)}, u32[]{:S(2)}) copy-start(bf16[34,64,128]{2,1,0:T(8,128)(2,1)} %param.10) | copy-start | bytes 1671172
  42.4 45.9 %copy-start.1 = (bf16[15,64,128]{2,1,0:T(8,128)(2,1)S(1)}, bf16[15,64,128]{2,1,0:T(8,128)(2,1)}, u32[]{:S(2)}) copy-start(bf16[15,64,128]{2,1,0:T(8,128)(2,1)} %param.13) | copy-start | bytes 737284
  42.4 46.0 %slice-start.1 = ((bf16[15,64,128]{2,1,0:T(8,128)(2,1)}), bf16[2,64,128]{2,1,0:T(8,128)(2,1)S(1)}, s32[]{:S(2)}) async-start(bf16[15,64,128]{2,1,0:T(8,128)(2,1)} %param.13), calls=%async_computation.18 | async-start | bytes 65536 | tf_op jit(solution)/shard_map/slice | solution.py:104
  47.9 22.2 %all-to-all-start.2 = ((bf16[8,5,64,128]{3,2,1,0:T(8,128)(2,1)}), bf16[8,5,64,128]{3,2,1,0:T(8,128)(2,1)S(1)}, u32[]{:S(2)}, u32[]{:S(2)}) async-start(bf16[8,5,64,128]{3,2,1,0:T(8,128)(2,1)} %constant_dynamic-update-slice_fusion), calls=%async_computation.2 | async-start | bytes 1310720 | tf_op jit(solution)/shard_map/all_to_all | solution.py:14
  51.4 102.0 %all-gather.22.cloned.1.call-start = ((), (), s32[]{:S(2)}) async-start(), calls=%async_computation.16 | async-start | bytes 12255232 | tf_op jit(solution)/shard_map/all_gather | solution.py:38
  89.2 17.0 %all-to-all-start.4 = ((bf16[4,5,64,128]{3,2,1,0:T(8,128)(2,1)}), bf16[4,5,64,128]{3,2,1,0:T(8,128)(2,1)S(1)}, u32[]{:S(2)}, u32[]{:S(2)}) async-start(bf16[4,5,64,128]{3,2,1,0:T(8,128)(2,1)} %copy.150), calls=%async_computation.4 | async-start | bytes 655360 | tf_op jit(solution)/shard_map/all_to_all | solution.py:14
  92.7 129.8 %all-gather.20.cloned.1.call-start = ((), (), s32[]{:S(2)}) async-start(), calls=%async_computation.15 | async-start | bytes 7798784 | tf_op jit(solution)/shard_map/all_gather | solution.py:38
  108.2 32.5 %all-to-all-start.5 = ((bf16[8,4,64,128]{3,2,1,0:T(8,128)(2,1)}), bf16[8,4,64,128]{3,2,1,0:T(8,128)(2,1)S(1)}, u32[]{:S(2)}, u32[]{:S(2)}) async-start(bf16[8,4,64,128]{3,2,1,0:T(8,128)(2,1)} %copy.154), calls=%async_computation.5 | async-start | bytes 1048576 | tf_op jit(solution)/shard_map/all_to_all | solution.py:14
  115.6 156.3 %all-gather.16.cloned.1.call-start = ((), (), s32[]{:S(2)}) async-start(), calls=%async_computation.13 | async-start | bytes 8912896 | tf_op jit(solution)/shard_map/all_gather | solution.py:38
  179.7 13.5 %all-to-all-start.7 = ((bf16[4,16,40,128]{3,2,1,0:T(8,128)(2,1)}), bf16[4,16,40,128]{3,2,1,0:T(8,128)(2,1)S(1)}, u32[]{:S(2)}, u32[]{:S(2)}) async-start(bf16[4,16,40,128]{3,2,1,0:T(8,128)(2,1)} %broadcast_in_dim.249), calls=%async_computation.7 | async-start | bytes 1310720 | tf_op jit(solution)/shard_map/all_to_all | solution.py:14
  250.3 12.5 %all-to-all-start.10 = ((bf16[4,16,40,128]{3,2,1,0:T(8,128)(2,1)}), bf16[4,16,40,128]{3,2,1,0:T(8,128)(2,1)S(1)}, u32[]{:S(2)}, u32[]{:S(2)}) async-start(bf16[4,16,40,128]{3,2,1,0:T(8,128)(2,1)} %broadcast_in_dim.252), calls=%async_computation.10 | async-start | bytes 1310720 | tf_op jit(solution)/shard_map/all_to_all | solution.py:14
  276.8 12.2 %all-to-all-start.11 = ((bf16[4,16,40,128]{3,2,1,0:T(8,128)(2,1)}), bf16[4,16,40,128]{3,2,1,0:T(8,128)(2,1)S(1)}, u32[]{:S(2)}, u32[]{:S(2)}) async-start(bf16[4,16,40,128]{3,2,1,0:T(8,128)(2,1)} %broadcast_in_dim.254), calls=%async_computation.11 | async-start | bytes 1310720 | tf_op jit(solution)/shard_map/all_to_all | solution.py:14
  292.8 13.6 %all-to-all-start.12 = ((bf16[8,2,3840]{2,1,0:T(2,128)(2,1)}), bf16[8,2,3840]{2,1,0:T(2,128)(2,1)S(1)}, u32[]{:S(2)}, u32[]{:S(2)}) async-start(bf16[8,2,3840]{2,1,0:T(2,128)(2,1)} %reshape.314), calls=%async_computation.12 | async-start | bytes 245760 | tf_op jit(solution)/shard_map/all_to_all | solution.py:14
Sparse Core Ops, SparseCore 0:
  32.9 46.1 all-gather.17
  81.3 72.1 all-gather.21
  155.6 52.3 all-gather.19
  210.0 57.3 all-gather.15

commit v4 on v3

--- a/solution.py
+++ b/solution.py
@@ -118,7 +118,7 @@
     node_part = by_rows(p_l1, v1).reshape(2, 4, 1, n, 64)
     part = (leaf_part + jnp.where(mine, node_part, 0.0)).astype(BF).reshape(2, 8, n, 64)
     quad = share(part, ("y1", "y0"), 4).astype(F32).reshape(4, 2, 8, n, 64).sum(0)
-    v2 = sum_x(by_cols(p_li2, (b2 - quad[0]).astype(BF))).astype(BF)
+    v2 = collect(by_cols(p_li2, (b2 - quad[0]).astype(BF)).astype(BF), "x").astype(BF)
 
     part = (parity(quad[1]) + by_rows(p_l23, v2)).astype(BF)
     update = share(part, ("y2", "y0"), 4).astype(F32).reshape(2, 2, 4, n, 64).sum(0)

time: 316 us -> 316 us (level)
  blocking collectives: 123 us -> 135 us
  waiting for transfers between devices: 71.1 us -> 62.9 us
    all_gather x7 -> x8, blocking collectives: 65.4 us -> 78.3 us  [collect(): return lax.all_gather(part, axis, axis=0, tiled=False).astype(F32).sum(0)]
    all_to_all x9 -> x8, waiting for transfers between devices: 65.3 us -> 57.2 us  [swap(): return lax.all_to_all(blocks, axes, 0, 0, tiled=True)]
    all_to_all x9 -> x8, starting transfers between devices: 44.6 us -> 41.6 us  [swap(): return lax.all_to_all(blocks, axes, 0, 0, tiled=True)]
  transfers between devices with their start and end apart: 13 -> 12, of which waited for: 8 -> 7; matrix products, arithmetic and copies ran while one was open for 15% -> 15% of each run, Pallas kernels for 0% -> 0%
where the time goes in v4:
time: 316 us; the launch traced here: 314 us
  blocking collectives  135 us (43%)
  waiting for transfers between devices  62.9 us (20%)
  starting transfers between devices  41.7 us (13%)
  matrix products  36 us (11%)
  local copies, waits for them, and re-layouts  15.5 us (5%)
  between operations  15.3 us (5%)
  other arithmetic  7.85 us (2%)
    all_gather x8, blocking collectives, collect(): return lax.all_gather(part, axis, axis=0, tiled=False).astype(F32).sum(0)  78.3 us
    all_to_all x8, waiting for transfers between devices, swap(): return lax.all_to_all(blocks, axes, 0, 0, tiled=True)  57.2 us
    all_to_all x4, blocking collectives, swap(): return lax.all_to_all(blocks, axes, 0, 0, tiled=True)  51.2 us
    all_to_all x8, starting transfers between devices, swap(): return lax.all_to_all(blocks, axes, 0, 0, tiled=True)  41.6 us
    dot_general x8, matrix products, by_rows(): jnp.einsum('pnc,psrc->snr', vector, panel, preferred_element_type=F32)  20.5 us
    dot_general x7, matrix products, by_cols(): jnp.einsum('snr,psrc->pnc', vector, panel, preferred_element_type=F32)  15.5 us
  transfers between devices with their start and end apart: 12, of which 7 were waited for; matrix products, arithmetic and copies ran while one was open for 15% of the time, Pallas kernels for 0%

profile of v4, /device:TPU:2, one launch (start us, length us, event | category | flops | bytes accessed | tf_op | source)
XLA Modules:
  0.0 313.9 jit_solution(10743978936379774345)
XLA Ops:
  10.0 7.2 %all-to-all-start = ((bf16[8,3,64,128]{3,2,1,0:T(8,128)(2,1)}), bf16[8,3,64,128]{3,2,1,0:T(8,128)(2,1)S(1)}, u32[]{:S(2)}, u32[]{:S(2)}) async-start(bf16[8,3,64,128]{3,2,1,0:T(8,128)(2,1)} %pad_maximum_fusion.3), calls=%async_computation | async-start | bytes 786432 | tf_op jit(solution)/shard_map/all_to_all | solution.py:14
  17.3 14.6 %all-to-all-done = bf16[8,3,64,128]{3,2,1,0:T(8,128)(2,1)S(1)} async-done(((bf16[8,3,64,128]{3,2,1,0:T(8,128)(2,1)}), bf16[8,3,64,128]{3,2,1,0:T(8,128)(2,1)S(1)}, u32[]{:S(2)}, u32[]{:S(2)}) %all-to-all-start) | async-done | bytes 393248 | tf_op jit(solution)/shard_map/all_to_all | solution.py:14
  42.4 5.5 %all-to-all-done.3 = bf16[4,3,64,128]{3,2,1,0:T(8,128)(2,1)S(1)} async-done(((bf16[4,3,64,128]{3,2,1,0:T(8,128)(2,1)}), bf16[4,3,64,128]{3,2,1,0:T(8,128)(2,1)S(1)}, u32[]{:S(2)}, u32[]{:S(2)}) %all-to-all-start.3) | async-done | bytes 196640 | tf_op jit(solution)/shard_map/all_to_all | solution.py:14
  51.5 18.6 %all-to-all-done.2 = bf16[8,5,64,128]{3,2,1,0:T(8,128)(2,1)S(1)} async-done(((bf16[8,5,64,128]{3,2,1,0:T(8,128)(2,1)}), bf16[8,5,64,128]{3,2,1,0:T(8,128)(2,1)S(1)}, u32[]{:S(2)}, u32[]{:S(2)}) %all-to-all-start.2) | async-done | bytes 655392 | tf_op jit(solution)/shard_map/all_to_all | solution.py:14
  71.6 11.8 %all_to_all.60 = bf16[8,2,5120]{2,1,0:T(2,128)(2,1)S(1)} all-to-all(bf16[8,2,5120]{2,1,0:T(2,128)(2,1)S(1)} %reshape.308), channel_id=1, replica_groups=mesh['z'=8,'core'=2,'x'=4,'y2'=2,'y1'=2,'y0'=2] {'y2','y1','y0'}, dimensions={0} | all-to-all | bytes 327680 | tf_op jit(solution)/shard_map/all_to_all | solution.py:14
  92.9 13.4 %all-gather.1 = bf16[64,40,128]{2,1,0:T(8,128)(2,1)S(1)} all-gather(bf16[16,40,128]{2,1,0:T(8,128)(2,1)S(1)} %fusion.13), channel_id=3, replica_groups=mesh['z'=8,'core'=2,'x'=4,'y2'=2,'y1'=2,'y0'=2] {'x'}, dimensions={0}, use_global_device_ids=true | all-gather | bytes 819200 | tf_op jit(solution)/shard_map/all_gather | solution.py:50
  108.3 7.5 %all-to-all-start.5 = ((bf16[8,4,64,128]{3,2,1,0:T(8,128)(2,1)}), bf16[8,4,64,128]{3,2,1,0:T(8,128)(2,1)S(1)}, u32[]{:S(2)}, u32[]{:S(2)}) async-start(bf16[8,4,64,128]{3,2,1,0:T(8,128)(2,1)} %copy.154), calls=%async_computation.5 | async-start | bytes 1048576 | tf_op jit(solution)/shard_map/all_to_all | solution.py:14
  118.6 7.5 %all-gather.2 = bf16[16,40,64]{2,1,0:T(8,128)(2,1)S(1)} all-gather(bf16[8,40,64]{2,1,0:T(8,128)(2,1)S(1)} %fusion.18), channel_id=4, replica_groups=mesh['z'=8,'core'=2,'x'=4,'y2'=2,'y1'=2,'y0'=2] {'y0'}, dimensions={0}, use_global_device_ids=true | all-gather | bytes 122880 | tf_op jit(solution)/shard_map/all_gather | solution.py:50
  127.7 13.0 %all-gather.3 = bf16[64,40,128]{2,1,0:T(8,128)(2,1)S(1)} all-gather(bf16[16,40,128]{2,1,0:T(8,128)(2,1)S(1)} %fusion.12), channel_id=5, replica_groups=mesh['z'=8,'core'=2,'x'=4,'y2'=2,'y1'=2,'y0'=2] {'x'}, dimensions={0}, use_global_device_ids=true | all-gather | bytes 819200 | tf_op jit(solution)/shard_map/all_gather | solution.py:50
  141.8 6.0 %all-gather.5 = bf16[32,40,128]{2,1,0:T(8,128)(2,1)S(1)} all-gather(bf16[16,40,128]{2,1,0:T(8,128)(2,1)S(1)} %reduce_sum.140), channel_id=7, replica_groups=mesh['z'=8,'core'=2,'x'=4,'y2'=2,'y1'=2,'y0'=2] {'y0'}, dimensions={0}, use_global_device_ids=true | all-gather | bytes 491520 | tf_op jit(solution)/shard_map/all_gather | solution.py:50
  147.9 5.6 %all-gather.23.cloned.1.call-done = bf16[704,64,128]{2,1,0:T(8,128)(2,1)} async-done(((bf16[44,64,128]{2,1,0:T(8,128)(2,1)}), bf16[704,64,128]{2,1,0:T(8,128)(2,1)}) %all-gather.23.cloned.1.call-update) | async-done | bytes 11534352 | tf_op jit(solution)/shard_map/all_gather | solution.py:38
  161.0 15.1 %all_to_all.61 = bf16[4,2,20480]{2,1,0:T(2,128)(2,1)S(1)} all-to-all(bf16[4,2,20480]{2,1,0:T(2,128)(2,1)S(1)} %reshape.310), channel_id=1, replica_groups=mesh['z'=8,'core'=2,'x'=4,'y2'=2,'y1'=2,'y0'=2] {'y1','y0'}, dimensions={0} | all-to-all | bytes 655360 | tf_op jit(solution)/shard_map/all_to_all | solution.py:14
  178.8 13.9 %all-gather.7 = bf16[64,40,128]{2,1,0:T(8,128)(2,1)S(1)} all-gather(bf16[16,40,128]{2,1,0:T(8,128)(2,1)S(1)} %fusion.11), channel_id=9, replica_groups=mesh['z'=8,'core'=2,'x'=4,'y2'=2,'y1'=2,'y0'=2] {'x'}, dimensions={0}, use_global_device_ids=true | all-gather | bytes 819200 | tf_op jit(solution)/shard_map/all_gather | solution.py:50
  194.8 12.6 %all_to_all.62 = bf16[4,2,5120]{2,1,0:T(2,128)(2,1)S(1)} all-to-all(bf16[4,2,5120]{2,1,0:T(2,128)(2,1)S(1)} %reshape.312), channel_id=1, replica_groups=mesh['z'=8,'core'=2,'x'=4,'y2'=2,'y1'=2,'y0'=2] {'y2','y0'}, dimensions={0} | all-to-all | bytes 163840 | tf_op jit(solution)/shard_map/all_to_all | solution.py:14
  209.9 11.6 %all_to_all.63 = bf16[4,16,40,128]{3,2,1,0:T(8,128)(2,1)S(1)} all-to-all(bf16[4,16,40,128]{3,2,1,0:T(8,128)(2,1)S(1)} %broadcast_in_dim.244), channel_id=1, replica_groups=mesh['z'=8,'core'=2,'x'=4,'y2'=2,'y1'=2,'y0'=2] {'x'}, dimensions={0} | all-to-all | bytes 1310720 | tf_op jit(solution)/shard_map/all_to_all | solution.py:14
  225.2 12.3 %all-gather.8 = bf16[64,40,128]{2,1,0:T(8,128)(2,1)S(1)} all-gather(bf16[16,40,128]{2,1,0:T(8,128)(2,1)S(1)} %fusion.9), channel_id=10, replica_groups=mesh['z'=8,'core'=2,'x'=4,'y2'=2,'y1'=2,'y0'=2] {'x'}, dimensions={0}, use_global_device_ids=true | all-gather | bytes 819200 | tf_op jit(solution)/shard_map/all_gather | solution.py:50
  237.6 6.0 %all-gather.9 = bf16[32,40,128]{2,1,0:T(8,128)(2,1)S(1)} all-gather(bf16[16,40,128]{2,1,0:T(8,128)(2,1)S(1)} %reduce_sum.146), channel_id=11, replica_groups=mesh['z'=8,'core'=2,'x'=4,'y2'=2,'y1'=2,'y0'=2] {'y0'}, dimensions={0}, use_global_device_ids=true | all-gather | bytes 491520 | tf_op jit(solution)/shard_map/all_gather | solution.py:50
  248.6 5.7 %all-to-all-start.9 = ((bf16[4,16,40,128]{3,2,1,0:T(8,128)(2,1)}), bf16[4,16,40,128]{3,2,1,0:T(8,128)(2,1)S(1)}, u32[]{:S(2)}, u32[]{:S(2)}) async-start(bf16[4,16,40,128]{3,2,1,0:T(8,128)(2,1)} %broadcast_in_dim.245), calls=%async_computation.9 | async-start | bytes 1310720 | tf_op jit(solution)/shard_map/all_to_all | solution.py:14
  254.3 5.1 %all-gather.10 = bf16[4,4,40,64]{3,2,1,0:T(8,128)(2,1)S(1)} all-gather(bf16[2,4,40,64]{3,2,1,0:T(8,128)(2,1)S(1)} %pad_maximum_fusion.9), channel_id=12, replica_groups=mesh['z'=8,'core'=2,'x'=4,'y2'=2,'y1'=2,'y0'=2] {'y0'}, dimensions={0}, use_global_device_ids=true | all-gather | bytes 122880 | tf_op jit(solution)/shard_map/all_gather | solution.py:136
  261.7 6.2 %all-gather.11 = bf16[32,40,128]{2,1,0:T(8,128)(2,1)S(1)} all-gather(bf16[16,40,128]{2,1,0:T(8,128)(2,1)S(1)} %reduce_sum.148), channel_id=13, replica_groups=mesh['z'=8,'core'=2,'x'=4,'y2'=2,'y1'=2,'y0'=2] {'y0'}, dimensions={0}, use_global_device_ids=true | all-gather | bytes 491520 | tf_op jit(solution)/shard_map/all_gather | solution.py:50
  275.6 4.9 %all-to-all-start.10 = ((bf16[4,16,40,128]{3,2,1,0:T(8,128)(2,1)}), bf16[4,16,40,128]{3,2,1,0:T(8,128)(2,1)S(1)}, u32[]{:S(2)}, u32[]{:S(2)}) async-start(bf16[4,16,40,128]{3,2,1,0:T(8,128)(2,1)} %broadcast_in_dim.247), calls=%async_computation.10 | async-start | bytes 1310720 | tf_op jit(solution)/shard_map/all_to_all | solution.py:14
  280.6 7.3 %all-to-all-done.10 = bf16[4,16,40,128]{3,2,1,0:T(8,128)(2,1)S(1)} async-done(((bf16[4,16,40,128]{3,2,1,0:T(8,128)(2,1)}), bf16[4,16,40,128]{3,2,1,0:T(8,128)(2,1)S(1)}, u32[]{:S(2)}, u32[]{:S(2)}) %all-to-all-start.10) | async-done | bytes 655392 | tf_op jit(solution)/shard_map/all_to_all | solution.py:14
  291.6 5.9 %all-to-all-start.11 = ((bf16[8,2,3840]{2,1,0:T(2,128)(2,1)}), bf16[8,2,3840]{2,1,0:T(2,128)(2,1)S(1)}, u32[]{:S(2)}, u32[]{:S(2)}) async-start(bf16[8,2,3840]{2,1,0:T(2,128)(2,1)} %reshape.314), calls=%async_computation.11 | async-start | bytes 245760 | tf_op jit(solution)/shard_map/all_to_all | solution.py:14
  297.4 9.0 %all-to-all-done.11 = bf16[8,2,3840]{2,1,0:T(2,128)(2,1)S(1)} async-done(((bf16[8,2,3840]{2,1,0:T(2,128)(2,1)}), bf16[8,2,3840]{2,1,0:T(2,128)(2,1)S(1)}, u32[]{:S(2)}, u32[]{:S(2)}) %all-to-all-start.11) | async-done | bytes 122912 | tf_op jit(solution)/shard_map/all_to_all | solution.py:14
  (158 shorter events, 72.2 us)
Async XLA Ops:
  6.5 33.8 %slice-start.2 = ((bf16[15,64,128]{2,1,0:T(8,128)(2,1)}), bf16[2,64,128]{2,1,0:T(8,128)(2,1)S(1)}, s32[]{:S(2)}) async-start(bf16[15,64,128]{2,1,0:T(8,128)(2,1)} %param.12), calls=%async_computation.18 | async-start | bytes 65536 | tf_op jit(solution)/shard_map/slice | solution.py:92
  6.5 34.5 %copy-start.2 = (bf16[15,64,128]{2,1,0:T(8,128)(2,1)S(1)}, bf16[15,64,128]{2,1,0:T(8,128)(2,1)}, u32[]{:S(2)}) copy-start(bf16[15,64,128]{2,1,0:T(8,128)(2,1)} %param.12) | copy-start | bytes 737284
  6.5 35.2 %slice-start = ((bf16[15,64,128]{2,1,0:T(8,128)(2,1)}), bf16[4,64,128]{2,1,0:T(8,128)(2,1)S(1)}, s32[]{:S(2)}) async-start(bf16[15,64,128]{2,1,0:T(8,128)(2,1)} %param.13), calls=%async_computation.16 | async-start | bytes 131072 | tf_op jit(solution)/shard_map/slice | solution.py:93
  10.0 61.1 %copy-start.3 = (bf16[15,64,40]{1,2,0:T(8,128)(2,1)S(1)}, bf16[15,64,40]{1,2,0:T(8,128)(2,1)}, u32[]{:S(2)}) copy-start(bf16[15,64,40]{1,2,0:T(8,128)(2,1)} %param.7) | copy-start | bytes 230404
  10.0 21.9 %all-to-all-start = ((bf16[8,3,64,128]{3,2,1,0:T(8,128)(2,1)}), bf16[8,3,64,128]{3,2,1,0:T(8,128)(2,1)S(1)}, u32[]{:S(2)}, u32[]{:S(2)}) async-start(bf16[8,3,64,128]{3,2,1,0:T(8,128)(2,1)} %pad_maximum_fusion.3), calls=%async_computation | async-start | bytes 786432 | tf_op jit(solution)/shard_map/all_to_all | solution.py:14
  17.3 68.9 %all-gather.19.cloned.1.call-start = ((), (), s32[]{:S(2)}) async-start(), calls=%async_computation.13 | async-start | bytes 5570560 | tf_op jit(solution)/shard_map/all_gather | solution.py:38
  35.6 12.3 %all-to-all-start.3 = ((bf16[4,3,64,128]{3,2,1,0:T(8,128)(2,1)}), bf16[4,3,64,128]{3,2,1,0:T(8,128)(2,1)S(1)}, u32[]{:S(2)}, u32[]{:S(2)}) async-start(bf16[4,3,64,128]{3,2,1,0:T(8,128)(2,1)} %copy.148), calls=%async_computation.3 | async-start | bytes 393216 | tf_op jit(solution)/shard_map/all_to_all | solution.py:14
  39.6 48.7 %copy-start.4 = (s32[34,1,2]{0,2,1:T(2,128)S(1)}, s32[34,1,2]{0,2,1:T(2,128)}, u32[]{:S(2)}) copy-start(s32[34,1,2]{0,2,1:T(2,128)} %param.11) | copy-start | bytes 820
  39.6 48.8 %copy-start = (bf16[34,64,128]{2,1,0:T(8,128)(2,1)S(1)}, bf16[34,64,128]{2,1,0:T(8,128)(2,1)}, u32[]{:S(2)}) copy-start(bf16[34,64,128]{2,1,0:T(8,128)(2,1)} %param.10) | copy-start | bytes 1671172
  42.4 46.1 %copy-start.1 = (bf16[15,64,128]{2,1,0:T(8,128)(2,1)S(1)}, bf16[15,64,128]{2,1,0:T(8,128)(2,1)}, u32[]{:S(2)}) copy-start(bf16[15,64,128]{2,1,0:T(8,128)(2,1)} %param.13) | copy-start | bytes 737284
  42.4 46.1 %slice-start.1 = ((bf16[15,64,128]{2,1,0:T(8,128)(2,1)}), bf16[2,64,128]{2,1,0:T(8,128)(2,1)S(1)}, s32[]{:S(2)}) async-start(bf16[15,64,128]{2,1,0:T(8,128)(2,1)} %param.13), calls=%async_computation.17 | async-start | bytes 65536 | tf_op jit(solution)/shard_map/slice | solution.py:104
  47.9 22.2 %all-to-all-start.2 = ((bf16[8,5,64,128]{3,2,1,0:T(8,128)(2,1)}), bf16[8,5,64,128]{3,2,1,0:T(8,128)(2,1)S(1)}, u32[]{:S(2)}, u32[]{:S(2)}) async-start(bf16[8,5,64,128]{3,2,1,0:T(8,128)(2,1)} %constant_dynamic-update-slice_fusion), calls=%async_computation.2 | async-start | bytes 1310720 | tf_op jit(solution)/shard_map/all_to_all | solution.py:14
  51.4 102.0 %all-gather.23.cloned.1.call-start = ((), (), s32[]{:S(2)}) async-start(), calls=%async_computation.15 | async-start | bytes 12255232 | tf_op jit(solution)/shard_map/all_gather | solution.py:38
  89.4 17.0 %all-to-all-start.4 = ((bf16[4,5,64,128]{3,2,1,0:T(8,128)(2,1)}), bf16[4,5,64,128]{3,2,1,0:T(8,128)(2,1)S(1)}, u32[]{:S(2)}, u32[]{:S(2)}) async-start(bf16[4,5,64,128]{3,2,1,0:T(8,128)(2,1)} %copy.150), calls=%async_computation.4 | async-start | bytes 655360 | tf_op jit(solution)/shard_map/all_to_all | solution.py:14
  92.8 128.8 %all-gather.21.cloned.1.call-start = ((), (), s32[]{:S(2)}) async-start(), calls=%async_computation.14 | async-start | bytes 7798784 | tf_op jit(solution)/shard_map/all_gather | solution.py:38
  108.3 32.5 %all-to-all-start.5 = ((bf16[8,4,64,128]{3,2,1,0:T(8,128)(2,1)}), bf16[8,4,64,128]{3,2,1,0:T(8,128)(2,1)S(1)}, u32[]{:S(2)}, u32[]{:S(2)}) async-start(bf16[8,4,64,128]{3,2,1,0:T(8,128)(2,1)} %copy.154), calls=%async_computation.5 | async-start | bytes 1048576 | tf_op jit(solution)/shard_map/all_to_all | solution.py:14
  115.8 154.9 %all-gather.17.cloned.1.call-start = ((), (), s32[]{:S(2)}) async-start(), calls=%async_computation.12 | async-start | bytes 8912896 | tf_op jit(solution)/shard_map/all_gather | solution.py:38
  248.6 13.1 %all-to-all-start.9 = ((bf16[4,16,40,128]{3,2,1,0:T(8,128)(2,1)}), bf16[4,16,40,128]{3,2,1,0:T(8,128)(2,1)S(1)}, u32[]{:S(2)}, u32[]{:S(2)}) async-start(bf16[4,16,40,128]{3,2,1,0:T(8,128)(2,1)} %broadcast_in_dim.245), calls=%async_computation.9 | async-start | bytes 1310720 | tf_op jit(solution)/shard_map/all_to_all | solution.py:14
  275.6 12.2 %all-to-all-start.10 = ((bf16[4,16,40,128]{3,2,1,0:T(8,128)(2,1)}), bf16[4,16,40,128]{3,2,1,0:T(8,128)(2,1)S(1)}, u32[]{:S(2)}, u32[]{:S(2)}) async-start(bf16[4,16,40,128]{3,2,1,0:T(8,128)(2,1)} %broadcast_in_dim.247), calls=%async_computation.10 | async-start | bytes 1310720 | tf_op jit(solution)/shard_map/all_to_all | solution.py:14
  291.6 14.8 %all-to-all-start.11 = ((bf16[8,2,3840]{2,1,0:T(2,128)(2,1)}), bf16[8,2,3840]{2,1,0:T(2,128)(2,1)S(1)}, u32[]{:S(2)}, u32[]{:S(2)}) async-start(bf16[8,2,3840]{2,1,0:T(2,128)(2,1)} %reshape.314), calls=%async_computation.11 | async-start | bytes 245760 | tf_op jit(solution)/shard_map/all_to_all | solution.py:14
Sparse Core Ops, SparseCore 0:
  33.0 46.1 all-gather.18
  81.3 72.1 all-gather.22
  155.6 52.3 all-gather.20
  210.0 57.3 all-gather.16
